TPU v7x, 32 devices: a whole 2x2x4 slice. The times are simulated.
32 devices in a mesh: fsdp: 8 (over y, x, core), dp: 4 (over z).
Axes of the slice: x: 2, y: 2, z: 4, core: 2. Of those that a mesh axis runs over, the one named last changes fastest.
Arguments:
- target: bfloat16 [32, 1024, 768], P(('fsdp', 'dp')), may hold values from -6 to 6
- memory: bfloat16 [32, 1024, 768], P(('fsdp', 'dp')), may hold values from -6 to 6
- target_lengths: int32 [32], P(('fsdp', 'dp')), may hold values from 256 to 1024, as said below
- memory_lengths: int32 [32], P(('fsdp', 'dp')), may hold values from 256 to 1024, as said below
- self_qkv: bfloat16 [3, 768, 768], P(None, 'fsdp'), may hold values from -0.21875 to 0.21875
- self_bias: bfloat16 [3, 768], P(None, 'fsdp'), may hold values from -3 to 3
- self_out: bfloat16 [768, 768], P('fsdp'), may hold values from -0.875 to 0.875
- cross_qkv: bfloat16 [3, 768, 768], P(None, 'fsdp'), may hold values from -0.21875 to 0.21875
- cross_bias: bfloat16 [3, 768], P(None, 'fsdp'), may hold values from -3 to 3
- cross_out: bfloat16 [768, 768], P('fsdp'), may hold values from -0.875 to 0.875
- ffn_in: bfloat16 [768, 3072], P('fsdp'), may hold values from -0.21875 to 0.21875
- ffn_in_bias: bfloat16 [3072], P('fsdp'), may hold values from -3 to 3
- ffn_out: bfloat16 [3072, 768], P('fsdp'), may hold values from -0.109375 to 0.109375
- ffn_out_bias: bfloat16 [768], P('fsdp'), may hold values from -3 to 3
- norm_gain: bfloat16 [3, 768], P(None, 'fsdp'), may hold values from 0.5 to 1.5
- norm_bias: bfloat16 [3, 768], P(None, 'fsdp'), may hold values from -3 to 3
- cotangent: bfloat16 [32, 1024, 768], P(('fsdp', 'dp')), may hold values from -6 to 6
Outputs:
- mixed: bfloat16 [32, 1024, 768], P(('fsdp', 'dp'))
- target_grad: float32 [32, 1024, 768], P(('fsdp', 'dp'))
- memory_grad: float32 [32, 1024, 768], P(('fsdp', 'dp'))
- self_qkv_grad: float32 [3, 768, 768], P(None, 'fsdp')
- self_bias_grad: float32 [3, 768], P(None, 'fsdp')
- self_out_grad: float32 [768, 768], P('fsdp')
- cross_qkv_grad: float32 [3, 768, 768], P(None, 'fsdp')
- cross_bias_grad: float32 [3, 768], P(None, 'fsdp')
- cross_out_grad: float32 [768, 768], P('fsdp')
- ffn_in_grad: float32 [768, 3072], P('fsdp')
- ffn_in_bias_grad: float32 [3072], P('fsdp')
- ffn_out_grad: float32 [3072, 768], P('fsdp')
- ffn_out_bias_grad: float32 [768], P('fsdp')
- norm_gain_grad: float32 [3, 768], P(None, 'fsdp')
- norm_bias_grad: float32 [3, 768], P(None, 'fsdp')
Inputs may be any that keep to these rules, and one draw needn't show every extreme that they name: `target_lengths`: real target tokens of each row; some row has all 1024. Queries past a row's length still produce outputs. `memory_lengths`: real memory tokens of each row; some row has all 1024.
All inputs are finite; a program needn't handle non-finite values.
Results may differ from a plain program's by a relative error of at most 0.025.
Values may be sent and summed in bfloat16 or wider, within the bound.
No kernel may reach another device: no remote copies, remote signals or barrier semaphores. Data moves between devices by JAX's collectives and lax.ppermute only.
A program may use at most 448 MiB of HBM per device.

v0:
```python
import jax
import jax.numpy as jnp
from jax import lax
from jax.sharding import PartitionSpec as P

HEADS = 12
HDIM = 64


def matmul(left, right):
    return jnp.dot(left, right, preferred_element_type=jnp.float32)


def matmul_tn(left, right):
    return lax.dot_general(
        left, right, (((0,), (0,)), ((), ())), preferred_element_type=jnp.float32
    )


def matmul_nt(left, right):
    return lax.dot_general(
        left, right, (((1,), (1,)), ((), ())), preferred_element_type=jnp.float32
    )


def exact_gelu(values):
    return jax.nn.gelu(values, approximate=False)


def split_heads(values):
    return values.reshape(values.shape[0], HEADS, HDIM).transpose(1, 0, 2)


def join_heads(values):
    return values.transpose(1, 0, 2).reshape(values.shape[1], HEADS * HDIM)


def make_masks(target_row, memory_row, target_len, memory_len):
    positions = jnp.arange(target_row.shape[0], dtype=jnp.int32)
    sources = jnp.arange(memory_row.shape[0], dtype=jnp.int32)
    self_allowed = (positions[None, :] <= positions[:, None]) & (positions[None, :] < target_len)
    cross_allowed = jnp.broadcast_to(
        sources[None, :] < memory_len, (positions.shape[0], sources.shape[0])
    )
    return (self_allowed, cross_allowed)


def norm_forward(summed, gain, shift):
    centred = summed - jnp.mean(summed, axis=-1, keepdims=True)
    inverse = lax.rsqrt(jnp.mean(centred * centred, axis=-1, keepdims=True) + 1e-05)
    normed = centred * inverse
    return (normed * gain.astype(jnp.float32) + shift.astype(jnp.float32), (normed, inverse))


def norm_backward(d_out, saved, gain):
    normed, inverse = saved
    d_normed = d_out * gain.astype(jnp.float32)
    d_in = inverse * (
        d_normed
        - jnp.mean(d_normed, axis=-1, keepdims=True)
        - normed * jnp.mean(d_normed * normed, axis=-1, keepdims=True)
    )
    return (d_in, jnp.sum(d_out * normed, axis=0), jnp.sum(d_out, axis=0))


def attend_forward(query_in, source, weights, biases, out_weight, allowed):
    factor = HDIM ** (-0.5)
    queries = ((matmul(query_in, weights[0]) + biases[0]) * factor).astype(jnp.bfloat16)
    keys_all = matmul(source, weights[1]).astype(jnp.bfloat16)
    values_all = (matmul(source, weights[2]) + biases[1]).astype(jnp.bfloat16)
    scores = jnp.einsum(
        "hqd,hkd->hqk",
        split_heads(queries),
        split_heads(keys_all),
        preferred_element_type=jnp.float32,
    )
    scores = jnp.where(allowed[None], scores, -1000000000.0)
    highest = jnp.max(scores, axis=-1, keepdims=True)
    expo = jnp.exp(scores - highest)
    totals = jnp.sum(expo, axis=-1, keepdims=True)
    probs = (expo / totals).astype(jnp.bfloat16)
    log_total = highest + jnp.log(totals)
    mixed = jnp.einsum(
        "hqk,hkd->hqd", probs, split_heads(values_all), preferred_element_type=jnp.float32
    )
    mixed = join_heads(mixed).astype(jnp.bfloat16)
    branch = matmul(mixed, out_weight) + biases[2]
    return (branch, (queries, keys_all, values_all, log_total, mixed))


def attend_backward(query_in, source, weights, out_weight, allowed, kept, d_branch):
    queries, keys_all, values_all, log_total, mixed = kept
    factor = HDIM ** (-0.5)
    d_branch = d_branch.astype(jnp.bfloat16)
    grad_out = matmul_tn(mixed, d_branch)
    grad_bias_out = jnp.sum(d_branch.astype(jnp.float32), axis=0)
    d_mixed = split_heads(matmul_nt(d_branch, out_weight).astype(jnp.bfloat16))
    head_q = split_heads(queries)
    head_k = split_heads(keys_all)
    head_v = split_heads(values_all)
    scores = jnp.einsum("hqd,hkd->hqk", head_q, head_k, preferred_element_type=jnp.float32)
    scores = jnp.where(allowed[None], scores, -1000000000.0)
    probs = jnp.exp(scores - log_total)
    d_values = join_heads(
        jnp.einsum(
            "hqk,hqd->hkd", probs.astype(jnp.bfloat16), d_mixed, preferred_element_type=jnp.float32
        )
    ).astype(jnp.bfloat16)
    d_probs = jnp.einsum("hqd,hkd->hqk", d_mixed, head_v, preferred_element_type=jnp.float32)
    d_scores = (probs * (d_probs - jnp.sum(probs * d_probs, axis=-1, keepdims=True))).astype(
        jnp.bfloat16
    )
    d_queries = join_heads(
        jnp.einsum("hqk,hkd->hqd", d_scores, head_k, preferred_element_type=jnp.float32)
    ).astype(jnp.bfloat16)
    d_keys = join_heads(
        jnp.einsum("hqk,hqd->hkd", d_scores, head_q, preferred_element_type=jnp.float32)
    ).astype(jnp.bfloat16)
    grad_weights = jnp.stack(
        [
            matmul_tn(query_in, d_queries) * factor,
            matmul_tn(source, d_keys),
            matmul_tn(source, d_values),
        ]
    )
    grad_biases = jnp.stack(
        [
            jnp.sum(d_queries.astype(jnp.float32), axis=0) * factor,
            jnp.sum(d_values.astype(jnp.float32), axis=0),
            grad_bias_out,
        ]
    )
    d_query_in = matmul_nt(d_queries, weights[0]) * factor
    d_source = matmul_nt(d_keys, weights[1]) + matmul_nt(d_values, weights[2])
    return (d_query_in, d_source, grad_weights, grad_biases, grad_out)


def row_forward(gathered, target_row, memory_row, target_len, memory_len):
    (
        self_qkv,
        self_bias,
        self_out,
        cross_qkv,
        cross_bias,
        cross_out,
        ffn_in,
        ffn_in_bias,
        ffn_out,
        ffn_out_bias,
        norm_gain,
        norm_bias,
    ) = gathered
    self_allowed, cross_allowed = make_masks(target_row, memory_row, target_len, memory_len)
    branch_one, self_kept = attend_forward(
        target_row, target_row, self_qkv, self_bias, self_out, self_allowed
    )
    first_hidden, norm_one = norm_forward(
        target_row.astype(jnp.float32) + branch_one, norm_gain[0], norm_bias[0]
    )
    hidden_one = first_hidden.astype(jnp.bfloat16)
    branch_two, cross_kept = attend_forward(
        hidden_one, memory_row, cross_qkv, cross_bias, cross_out, cross_allowed
    )
    second_hidden, norm_two = norm_forward(first_hidden + branch_two, norm_gain[1], norm_bias[1])
    hidden_two = second_hidden.astype(jnp.bfloat16)
    pre_act = matmul(hidden_two, ffn_in) + ffn_in_bias
    activ = exact_gelu(pre_act).astype(jnp.bfloat16)
    final, norm_three = norm_forward(
        second_hidden + matmul(activ, ffn_out) + ffn_out_bias, norm_gain[2], norm_bias[2]
    )
    return (
        final,
        (
            self_kept,
            norm_one,
            hidden_one,
            cross_kept,
            norm_two,
            hidden_two,
            pre_act,
            activ,
            norm_three,
        ),
    )


def row_backward(gathered, target_row, memory_row, target_len, memory_len, kept, d_out):
    (
        self_qkv,
        self_bias,
        self_out,
        cross_qkv,
        cross_bias,
        cross_out,
        ffn_in,
        ffn_in_bias,
        ffn_out,
        ffn_out_bias,
        norm_gain,
        norm_bias,
    ) = gathered
    self_allowed, cross_allowed = make_masks(target_row, memory_row, target_len, memory_len)
    (
        self_kept,
        norm_one,
        hidden_one,
        cross_kept,
        norm_two,
        hidden_two,
        pre_act,
        activ,
        norm_three,
    ) = kept
    d_sum_three, gain_three, shift_three = norm_backward(d_out, norm_three, norm_gain[2])
    d_ffn = d_sum_three.astype(jnp.bfloat16)
    grad_ffn_out = matmul_tn(activ, d_ffn)
    grad_ffn_out_bias = jnp.sum(d_ffn.astype(jnp.float32), axis=0)
    d_activ = matmul_nt(d_ffn, ffn_out)
    gelu_back = jax.vjp(exact_gelu, pre_act)[1]
    d_pre = gelu_back(d_activ)[0].astype(jnp.bfloat16)
    grad_ffn_in = matmul_tn(hidden_two, d_pre)
    grad_ffn_in_bias = jnp.sum(d_pre.astype(jnp.float32), axis=0)
    d_hidden_two = d_sum_three + matmul_nt(d_pre, ffn_in)
    d_sum_two, gain_two, shift_two = norm_backward(d_hidden_two, norm_two, norm_gain[1])
    d_query_two, d_memory_row, cross_w, cross_b, cross_o = attend_backward(
        hidden_one, memory_row, cross_qkv, cross_out, cross_allowed, cross_kept, d_sum_two
    )
    d_hidden_one = d_sum_two + d_query_two
    d_sum_one, gain_one, shift_one = norm_backward(d_hidden_one, norm_one, norm_gain[0])
    d_query_one, d_source_one, self_w, self_b, self_o = attend_backward(
        target_row, target_row, self_qkv, self_out, self_allowed, self_kept, d_sum_one
    )
    d_target_row = d_sum_one + d_query_one + d_source_one
    grads = (
        self_w,
        self_b,
        self_o,
        cross_w,
        cross_b,
        cross_o,
        grad_ffn_in,
        grad_ffn_in_bias,
        grad_ffn_out,
        grad_ffn_out_bias,
        jnp.stack([gain_one, gain_two, gain_three]),
        jnp.stack([shift_one, shift_two, shift_three]),
    )
    return (d_target_row, d_memory_row, grads)


def shards(
    target,
    memory,
    target_lengths,
    memory_lengths,
    self_qkv,
    self_bias,
    self_out,
    cross_qkv,
    cross_bias,
    cross_out,
    ffn_in,
    ffn_in_bias,
    ffn_out,
    ffn_out_bias,
    norm_gain,
    norm_bias,
    cotangent,
):
    gathered = (
        lax.all_gather(self_qkv, "fsdp", axis=1, tiled=True),
        lax.all_gather(self_bias, "fsdp", axis=1, tiled=True),
        lax.all_gather(self_out, "fsdp", axis=0, tiled=True),
        lax.all_gather(cross_qkv, "fsdp", axis=1, tiled=True),
        lax.all_gather(cross_bias, "fsdp", axis=1, tiled=True),
        lax.all_gather(cross_out, "fsdp", axis=0, tiled=True),
        lax.all_gather(ffn_in, "fsdp", axis=0, tiled=True),
        lax.all_gather(ffn_in_bias, "fsdp", axis=0, tiled=True),
        lax.all_gather(ffn_out, "fsdp", axis=0, tiled=True),
        lax.all_gather(ffn_out_bias, "fsdp", axis=0, tiled=True),
        lax.all_gather(norm_gain, "fsdp", axis=1, tiled=True),
        lax.all_gather(norm_bias, "fsdp", axis=1, tiled=True),
    )
    inputs = (target, memory, target_lengths, memory_lengths)
    zero_grads = tuple((jnp.zeros(member.shape, jnp.float32) for member in gathered))
    outputs = lax.map(
        lambda packed: row_forward(gathered, packed[0], packed[1], packed[2], packed[3])[0], inputs
    )
    again = (
        lax.all_gather(self_qkv, "fsdp", axis=1, tiled=True),
        lax.all_gather(self_bias, "fsdp", axis=1, tiled=True),
        lax.all_gather(self_out, "fsdp", axis=0, tiled=True),
        lax.all_gather(cross_qkv, "fsdp", axis=1, tiled=True),
        lax.all_gather(cross_bias, "fsdp", axis=1, tiled=True),
        lax.all_gather(cross_out, "fsdp", axis=0, tiled=True),
        lax.all_gather(ffn_in, "fsdp", axis=0, tiled=True),
        lax.all_gather(ffn_in_bias, "fsdp", axis=0, tiled=True),
        lax.all_gather(ffn_out, "fsdp", axis=0, tiled=True),
        lax.all_gather(ffn_out_bias, "fsdp", axis=0, tiled=True),
        lax.all_gather(norm_gain, "fsdp", axis=1, tiled=True),
        lax.all_gather(norm_bias, "fsdp", axis=1, tiled=True),
    )

    def backward_step(totals, packed):
        kept = row_forward(again, packed[0], packed[1], packed[2], packed[3])[1]
        d_target_row, d_memory_row, grads = row_backward(
            again, packed[0], packed[1], packed[2], packed[3], kept, packed[4].astype(jnp.float32)
        )
        return (jax.tree.map(jnp.add, totals, grads), (d_target_row, d_memory_row))

    totals, (d_targets, d_memories) = lax.scan(backward_step, zero_grads, inputs + (cotangent,))
    reduced = (
        lax.psum_scatter(totals[0], "fsdp", scatter_dimension=1, tiled=True),
        lax.psum_scatter(totals[1], "fsdp", scatter_dimension=1, tiled=True),
        lax.psum_scatter(totals[2], "fsdp", scatter_dimension=0, tiled=True),
        lax.psum_scatter(totals[3], "fsdp", scatter_dimension=1, tiled=True),
        lax.psum_scatter(totals[4], "fsdp", scatter_dimension=1, tiled=True),
        lax.psum_scatter(totals[5], "fsdp", scatter_dimension=0, tiled=True),
        lax.psum_scatter(totals[6], "fsdp", scatter_dimension=0, tiled=True),
        lax.psum_scatter(totals[7], "fsdp", scatter_dimension=0, tiled=True),
        lax.psum_scatter(totals[8], "fsdp", scatter_dimension=0, tiled=True),
        lax.psum_scatter(totals[9], "fsdp", scatter_dimension=0, tiled=True),
        lax.psum_scatter(totals[10], "fsdp", scatter_dimension=1, tiled=True),
        lax.psum_scatter(totals[11], "fsdp", scatter_dimension=1, tiled=True),
    )
    summed = (
        lax.psum(reduced[0].astype(jnp.bfloat16), "dp").astype(jnp.float32),
        lax.psum(reduced[1].astype(jnp.bfloat16), "dp").astype(jnp.float32),
        lax.psum(reduced[2].astype(jnp.bfloat16), "dp").astype(jnp.float32),
        lax.psum(reduced[3].astype(jnp.bfloat16), "dp").astype(jnp.float32),
        lax.psum(reduced[4].astype(jnp.bfloat16), "dp").astype(jnp.float32),
        lax.psum(reduced[5].astype(jnp.bfloat16), "dp").astype(jnp.float32),
        lax.psum(reduced[6].astype(jnp.bfloat16), "dp").astype(jnp.float32),
        lax.psum(reduced[7].astype(jnp.bfloat16), "dp").astype(jnp.float32),
        lax.psum(reduced[8].astype(jnp.bfloat16), "dp").astype(jnp.float32),
        lax.psum(reduced[9].astype(jnp.bfloat16), "dp").astype(jnp.float32),
        lax.psum(reduced[10].astype(jnp.bfloat16), "dp").astype(jnp.float32),
        lax.psum(reduced[11].astype(jnp.bfloat16), "dp").astype(jnp.float32),
    )
    return (outputs.astype(jnp.bfloat16), d_targets, d_memories) + tuple(summed)


def solution(mesh):
    in_specs = (
        P(("fsdp", "dp"), None, None),
        P(("fsdp", "dp"), None, None),
        P(("fsdp", "dp")),
        P(("fsdp", "dp")),
        P(None, "fsdp", None),
        P(None, "fsdp"),
        P("fsdp", None),
        P(None, "fsdp", None),
        P(None, "fsdp"),
        P("fsdp", None),
        P("fsdp", None),
        P("fsdp"),
        P("fsdp", None),
        P("fsdp"),
        P(None, "fsdp"),
        P(None, "fsdp"),
        P(("fsdp", "dp"), None, None),
    )
    out_specs = (
        P(("fsdp", "dp"), None, None),
        P(("fsdp", "dp"), None, None),
        P(("fsdp", "dp"), None, None),
        P(None, "fsdp", None),
        P(None, "fsdp"),
        P("fsdp", None),
        P(None, "fsdp", None),
        P(None, "fsdp"),
        P("fsdp", None),
        P("fsdp", None),
        P("fsdp"),
        P("fsdp", None),
        P("fsdp"),
        P(None, "fsdp"),
        P(None, "fsdp"),
    )
    return jax.shard_map(shards, mesh=mesh, in_specs=in_specs, out_specs=out_specs, check_vma=False)
```

profile of v0, /device:TPU:0, one launch (start us, length us, event | category | flops | bytes accessed | tf_op | source)
XLA Modules:
  0.0 1165.7 jit_solution(12040859188325762577)
XLA Ops:
  16.1 15.3 %all-reduce = bf16[768]{0:T(1024)(128)(2,1)S(1)} all-reduce(bf16[768]{0:T(1024)(128)(2,1)S(1)} %dynamic-update-slice), channel_id=1, replica_groups=mesh['fsdp'=8,'dp'=4] {'fsdp'}, use_global_device_ids=true, to_apply=%add | all-reduce | flops 768 | bytes 3072
  32.0 7.8 all-gather
  39.9 9.0 all-gather.3
  49.6 8.0 all-gather.1
  58.4 8.7 all-gather.2
  67.8 8.0 all-gather.4
  76.8 3.0 copy.86
  82.4 4.5 convolution_convert_fusion.7
  86.9 3.9 multiply_convert_fusion.4
  90.8 21.5 %select_reduce_fusion.1 = (f32[12,1024]{1,0:T(8,128)S(1)}, f32[12,1024,1024]{1,2,0:T(8,128)}) fusion(pred[1024,1024]{0,1:T(8,128)(4,1)S(1)} %fusion.18, bf16[12,1024,64]{1,2,0:T(8,128)(2,1)} %bitcast.264, bf16[12,1024,64]{1,2,0:T(8,128)(2,1)} %bitcast.258), kind=kOutput, calls=%fused_computation.13 | convolution fusion | flops 1635766272 | bytes 54575104 | tf_op jit(solution)/shard_map/while/body/eval_jaxpr/hqd,hkd->hqk/dot_general | solution.py:71
  112.3 20.6 %fusion = f32[12,1024]{1,0:T(8,128)S(1)} fusion(f32[12,1024,1024]{1,2,0:T(8,128)} %get-tuple-element.259, f32[12,1024]{1,0:T(8,128)S(1)} %get-tuple-element.258, pred[1024,1024]{0,1:T(8,128)(4,1)S(1)} %fusion.18), kind=kLoop, calls=%fused_computation.10 | loop fusion | flops 37736448 | bytes 51478528 | tf_op jit(solution)/shard_map/while/body/eval_jaxpr/reduce_sum | solution.py:80
  133.5 2.7 add_convert_fusion.3
  137.4 21.4 %fusion.36 = bf16[12,1024,64]{1,2,0:T(8,128)(2,1)} fusion(bf16[12,1024,64]{1,2,0:T(8,128)(2,1)S(1)} %bitcast.271, f32[12,1024,1024]{1,2,0:T(8,128)} %get-tuple-element.259, f32[12,1024]{1,0:T(8,128)S(1)} %fusion, f32[12,1024]{1,0:T(8,128)S(1)} %get-tuple-element.258, pred[1024,1024]{0,1:T(8,128)(4,1)S(1)} %fusion.18), kind=kOutput, calls=%fused_computation.108 | convolution fusion | flops 1661730816 | bytes 54624256 | tf_op jit(solution)/shard_map/while/body/eval_jaxpr/hqk,hkd->hqd/dot_general | solution.py:83
  158.8 4.0 fusion.84
  164.9 2.9 convolution_convert_fusion.6
  167.8 4.7 multiply_convert_fusion.3
  172.4 22.4 %select_reduce_fusion = (f32[12,1024]{1,0:T(8,128)S(1)}, f32[12,1024,1024]{1,2,0:T(8,128)}) fusion(pred[1024]{0:T(1024)(128)(4,1)S(1)} %iota_compare_fusion.1, bf16[12,1024,64]{1,2,0:T(8,128)(2,1)} %bitcast.262, bf16[12,1024,64]{1,2,0:T(8,128)(2,1)S(1)} %bitcast.256), kind=kOutput, calls=%fused_computation.12 | convolution fusion | flops 1635766272 | bytes 53527552 | tf_op jit(solution)/shard_map/while/body/eval_jaxpr/hqd,hkd->hqk/dot_general | solution.py:71
  194.8 21.4 %fusion.1 = f32[12,1024]{1,0:T(8,128)S(1)} fusion(f32[12,1024,1024]{1,2,0:T(8,128)} %get-tuple-element.263, f32[12,1024]{1,0:T(8,128)S(1)} %get-tuple-element.262, pred[1024]{0:T(1024)(128)(4,1)S(1)} %iota_compare_fusion.1), kind=kLoop, calls=%fused_computation.11 | loop fusion | flops 37736448 | bytes 50430976 | tf_op jit(solution)/shard_map/while/body/eval_jaxpr/reduce_sum | solution.py:80
  220.7 20.0 %fusion.37 = bf16[12,1024,64]{1,2,0:T(8,128)(2,1)} fusion(bf16[12,1024,64]{1,2,0:T(8,128)(2,1)S(1)} %bitcast.273, f32[12,1024,1024]{1,2,0:T(8,128)} %get-tuple-element.263, f32[12,1024]{1,0:T(8,128)S(1)} %fusion.1, f32[12,1024]{1,0:T(8,128)S(1)} %get-tuple-element.262, pred[1024]{0:T(1024)(128)(4,1)S(1)} %iota_compare_fusion.1), kind=kOutput, calls=%fused_computation.109 | convolution fusion | flops 1661730816 | bytes 53576704 | tf_op jit(solution)/shard_map/while/body/eval_jaxpr/hqk,hkd->hqd/dot_general | solution.py:83
  240.8 4.7 fusion.85
  247.7 37.9 %multiply_convert_fusion.2 = (bf16[1024,3072]{1,0:T(8,128)(2,1)}, f32[1024,3072]{1,0:T(8,128)}, f32[1024,3072]{1,0:T(8,128)}) fusion(f32[3072]{0:T(1024)S(1)} %bitcast.289, bf16[768,3072]{1,0:T(8,128)(2,1)} %all-gather.20.cloned.1.call-done, f32[1024,768]{0,1:T(8,128)} %copy-done.9, f32[768]{0:T(1024)S(1)} %copy-done.73, f32[768]{0:T(1024)S(1)} %copy-done.59, ...), kind=kOutput, calls=%fused_computation.26 | convolution fusion | flops 5043388416 | bytes 39348224 | tf_op jit(solution)/shard_map/while/body/eval_jaxpr/dot_general | solution.py:11
  285.6 9.8 fusion.86
  298.7 3.5 convert_reduce_fusion.2
  302.2 18.9 %convert_reduce_fusion = (f32[3072]{0:T(1024)}, bf16[1024,3072]{1,0:T(8,128)(2,1)}) fusion(f32[1024,3072]{1,0:T(8,128)} %get-tuple-element.254, bf16[1024,768]{0,1:T(8,128)(2,1)} %get-tuple-element.248, bf16[3072,768]{1,0:T(8,128)(2,1)} %all-gather.22.cloned.1.call-done, f32[1024,3072]{1,0:T(8,128)} %get-tuple-element.266, f32[3072]{0:T(1024)S(1)} %bitcast.290), kind=kOutput, calls=%fused_computation.24 | convolution fusion | flops 4885312512 | bytes 37773312 | tf_op jit(solution)/shard_map/while/body/eval_jaxpr/dot_general | solution.py:21
  321.1 11.5 multiply_reduce_fusion.2
  336.0 2.8 fusion.68
  338.9 4.9 convolution_convert_fusion.3
  343.8 35.1 %multiply_reduce_fusion.1 = (f32[12,1024]{1,0:T(8,128)S(1)}, f32[12,1024,1024]{1,2,0:T(8,128)}) fusion(f32[12,1024,1024]{1,2,0:T(8,128)} %get-tuple-element.263, f32[12,1024]{1,0:T(8,128)S(1)} %copy-done.36, pred[1024]{0:T(1024)(128)(4,1)S(1)} %copy-done.42, bf16[12,1024,64]{1,2,0:T(8,128)(2,1)} %bitcast.277, bf16[12,1024,64]{1,2,0:T(8,128)(2,1)S(1)} %bitcast.274), kind=kOutput, calls=%fused_computation.4 | convolution fusion | flops 1660932096 | bytes 103908352 | tf_op jit(solution)/shard_map/while/body/eval_jaxpr/hqd,hkd->hqk/dot_general | solution.py:109
  378.9 40.4 %multiply_convert_fusion.1 = bf16[12,1024,1024]{1,2,0:T(8,128)(2,1)} fusion(f32[12,1024,1024]{1,2,0:T(8,128)} %get-tuple-element.271, f32[12,1024,1024]{1,2,0:T(8,128)} %get-tuple-element.263, f32[12,1024]{1,0:T(8,128)S(1)} %get-tuple-element.270, f32[12,1024]{1,0:T(8,128)S(1)} %copy-done.36, pred[1024]{0:T(1024)(128)(4,1)S(1)} %copy-done.42), kind=kLoop, calls=%fused_computation.3 | loop fusion | flops 62914560 | bytes 125928448 | tf_op jit(solution)/shard_map/while/body/eval_jaxpr/convert_element_type | solution.py:110
  419.4 13.5 %convert_reduce_fusion.5 = (f32[12,64]{1,0:T(8,128)}, bf16[12,1024,64]{1,2,0:T(8,128)(2,1)S(1)}) fusion(bf16[12,1024,64]{1,2,0:T(8,128)(2,1)S(1)} %bitcast.257, bf16[12,1024,1024]{1,2,0:T(8,128)(2,1)} %multiply_convert_fusion.1), kind=kOutput, calls=%fused_computation.60 | convolution fusion | flops 1612971264 | bytes 28314624 | tf_op jit(solution)/shard_map/while/body/eval_jaxpr/hqk,hkd->hqd/dot_general | solution.py:114
  432.9 4.8 multiply_reduce_fusion.3
  441.4 21.1 %convert_reduce_fusion.7 = (f32[12,64]{1,0:T(8,128)}, bf16[12,1024,64]{1,2,0:T(8,128)(2,1)}) fusion(bf16[12,1024,64]{1,2,0:T(8,128)(2,1)S(1)} %bitcast.279, f32[12,1024,1024]{1,2,0:T(8,128)} %get-tuple-element.259, f32[12,1024]{1,0:T(8,128)S(1)} %copy-done.37, pred[1024,1024]{0,1:T(8,128)(4,1)S(1)} %copy-done.2), kind=kOutput, calls=%fused_computation.62 | convolution fusion | flops 1650720000 | bytes 54578176 | tf_op jit(solution)/shard_map/while/body/eval_jaxpr/hqk,hqd->hkd/dot_general | solution.py:105
  462.5 2.9 fusion.65
  465.4 33.5 %multiply_reduce_fusion = (f32[12,1024]{1,0:T(8,128)S(1)}, f32[12,1024,1024]{1,2,0:T(8,128)}) fusion(f32[12,1024,1024]{1,2,0:T(8,128)} %get-tuple-element.259, f32[12,1024]{1,0:T(8,128)S(1)} %copy-done.37, pred[1024,1024]{0,1:T(8,128)(4,1)S(1)} %copy-done.2, bf16[12,1024,64]{1,2,0:T(8,128)(2,1)} %bitcast.280, bf16[12,1024,64]{1,2,0:T(8,128)(2,1)} %bitcast.272), kind=kOutput, calls=%fused_computation.1 | convolution fusion | flops 1660932096 | bytes 104955904 | tf_op jit(solution)/shard_map/while/body/eval_jaxpr/hqd,hkd->hqk/dot_general | solution.py:109
  499.0 42.9 %multiply_convert_fusion = bf16[12,1024,1024]{1,2,0:T(8,128)(2,1)} fusion(f32[12,1024,1024]{1,2,0:T(8,128)} %get-tuple-element.274, f32[12,1024,1024]{1,2,0:T(8,128)} %get-tuple-element.259, f32[12,1024]{1,0:T(8,128)S(1)} %get-tuple-element.273, f32[12,1024]{1,0:T(8,128)S(1)} %copy-done.37, pred[1024,1024]{0,1:T(8,128)(4,1)S(1)} %copy-done.2), kind=kLoop, calls=%fused_computation | loop fusion | flops 62914560 | bytes 126976000 | tf_op jit(solution)/shard_map/while/body/eval_jaxpr/convert_element_type | solution.py:110
  541.9 13.3 %convert_reduce_fusion.8 = (f32[12,64]{1,0:T(8,128)S(1)}, bf16[12,1024,64]{1,2,0:T(8,128)(2,1)S(1)}) fusion(bf16[12,1024,64]{1,2,0:T(8,128)(2,1)} %bitcast.259, bf16[12,1024,1024]{1,2,0:T(8,128)(2,1)} %multiply_convert_fusion), kind=kOutput, calls=%fused_computation.63 | convolution fusion | flops 1612971264 | bytes 28314624 | tf_op jit(solution)/shard_map/while/body/eval_jaxpr/hqk,hkd->hqd/dot_general | solution.py:114
  555.2 2.8 convolution_bitcast_fusion.2
  558.0 2.9 multiply_bitcast_fusion.1
  560.9 13.7 %convolution_convert_fusion.5 = bf16[12,1024,64]{1,2,0:T(8,128)(2,1)} fusion(bf16[12,1024,1024]{1,2,0:T(8,128)(2,1)} %multiply_convert_fusion, bf16[12,1024,64]{1,2,0:T(8,128)(2,1)S(1)} %bitcast.265), kind=kOutput, calls=%fused_computation.105 | convolution fusion | flops 1611399168 | bytes 28311552 | tf_op jit(solution)/shard_map/while/body/eval_jaxpr/hqk,hqd->hkd/dot_general | solution.py:117
  574.6 3.4 convolution_bitcast_fusion.3
  578.0 3.3 pad_maximum_fusion
  581.3 10.7 copy.119
  592.0 8.2 copy.129
  601.6 22.2 %convert_reduce_fusion.4 = (f32[12,64]{1,0:T(8,128)S(1)}, bf16[12,1024,64]{1,2,0:T(8,128)(2,1)S(1)}) fusion(bf16[12,1024,64]{1,2,0:T(8,128)(2,1)S(1)} %bitcast.278, f32[12,1024,1024]{1,2,0:T(8,128)} %get-tuple-element.263, f32[12,1024]{1,0:T(8,128)S(1)} %copy-done.36, pred[1024]{0:T(1024)(128)(4,1)S(1)} %copy-done.42), kind=kOutput, calls=%fused_computation.59 | convolution fusion | flops 1650720000 | bytes 53530624 | tf_op jit(solution)/shard_map/while/body/eval_jaxpr/hqk,hqd->hkd/dot_general | solution.py:105
  625.0 2.9 convolution_bitcast_fusion
  627.9 13.8 %convolution_convert_fusion.4 = bf16[12,1024,64]{1,2,0:T(8,128)(2,1)} fusion(bf16[12,1024,1024]{1,2,0:T(8,128)(2,1)} %multiply_convert_fusion.1, bf16[12,1024,64]{1,2,0:T(8,128)(2,1)S(1)} %bitcast.263), kind=kOutput, calls=%fused_computation.104 | convolution fusion | flops 1611399168 | bytes 28311552 | tf_op jit(solution)/shard_map/while/body/eval_jaxpr/hqk,hqd->hkd/dot_general | solution.py:117
  641.7 3.1 convolution_bitcast_fusion.1
  646.5 3.3 pad_maximum_fusion.1
  650.5 10.9 fusion.75
  662.8 10.3 fusion.87
  685.8 49.9 %reduce-scatter.23.cloned.1.call-done = f32[3,96,768]{2,1,0:T(8,128)} async-done(((f32[3,768,768]{2,1,0:T(8,128)}), f32[3,96,768]{2,1,0:T(8,128)}) %reduce-scatter.23.cloned.1.call-update) | async-done | bytes 884752 | tf_op jit(solution)/shard_map/reduce_scatter | solution.py:316
  737.6 78.0 %reduce-scatter.27.cloned.1.call-done = f32[96,3072]{1,0:T(8,128)} async-done(((f32[768,3072]{1,0:T(8,128)}), f32[96,3072]{1,0:T(8,128)}) %reduce-scatter.27.cloned.1.call-update) | async-done | bytes 1179664 | tf_op jit(solution)/shard_map/reduce_scatter | solution.py:319
  817.8 77.7 %reduce-scatter.29.cloned.1.call-done = f32[384,768]{1,0:T(8,128)} async-done(((f32[3072,768]{1,0:T(8,128)}), f32[384,768]{1,0:T(8,128)}) %reduce-scatter.29.cloned.1.call-update) | async-done | bytes 1179664 | tf_op jit(solution)/shard_map/reduce_scatter | solution.py:321
  900.6 3.3 fusion.49
  906.3 3.2 add_bitcast_fusion.1
  909.4 3.7 copy.101
  913.1 23.5 %all-reduce.3 = (bf16[3072]{0:T(1024)(128)(2,1)S(1)}, bf16[768]{0:T(1024)(128)(2,1)S(1)}) all-reduce(f32[3072]{0:T(1024)S(1)} %copy-done.66, f32[768]{0:T(1024)S(1)} %copy-done.58), channel_id=9, replica_groups=mesh['fsdp'=8,'dp'=4] {'fsdp'}, use_global_device_ids=true, to_apply=%region_39.40.clone | all-reduce | flops 3840 | bytes 23040
  936.8 2.9 fusion.51
  939.7 4.5 add_bitcast_fusion
  945.0 24.2 %reduce-scatter.37.cloned.1.call-done = f32[96,3]{1,0:T(8,128)} async-done(((f32[768,3]{1,0:T(8,128)}), f32[96,3]{1,0:T(8,128)}) %reduce-scatter.37.cloned.1.call-update) | async-done | bytes 1168
  970.1 35.9 %reduce-scatter.35.cloned.1.call-done = f32[96,3]{1,0:T(8,128)} async-done(((f32[768,3]{1,0:T(8,128)}), f32[96,3]{1,0:T(8,128)}) %reduce-scatter.35.cloned.1.call-update) | async-done | bytes 1168
  1006.8 35.9 %reduce-scatter.33.cloned.1.call-done = f32[96,3]{1,0:T(8,128)} async-done(((f32[768,3]{1,0:T(8,128)}), f32[96,3]{1,0:T(8,128)}) %reduce-scatter.33.cloned.1.call-update) | async-done | bytes 1168
  1043.6 12.0 %all-reduce.4 = (bf16[3,96]{1,0:T(4,128)(2,1)S(1)}, bf16[3,96]{1,0:T(4,128)(2,1)S(1)}, bf16[384]{0:T(512)(128)(2,1)S(1)}, bf16[96]{0:T(256)(128)(2,1)S(1)}, bf16...) all-reduce(bf16[3,96]{1,0:T(4,128)(2,1)S(1)} %copy.122, ...), channel_id=1, replica_groups=mesh['fsdp'=8,'dp'=4] {'dp'}, use_global_device_ids=true, to_apply=%region_24.25 | all-reduce | flops 1632 | bytes 6528 | tf_op jit(solution)/shard_map/psum | solution.py:328
  1059.0 90.0 %all-reduce.8.cloned.1.call-done = (bf16[3,96,768]{1,2,0:T(8,128)(2,1)}, bf16[96,768]{1,0:T(8,128)(2,1)}, bf16[3,96,768]{2,1,0:T(8,128)(2,1)}, bf16[96,768]{1,0:...) async-done(((bf16[3,96,768]{1,2,0:T(8,128)(2,1)}, bf16[96,768]{1,0:T(8,128)(2,1)}, bf16[3,96,768]{2,1,0:T(8,128)(2,1)}, bf16[96,768]{1,0:T(8,128)(2,1)}, ...) | async-done | bytes 2359312 | tf_op jit(solution)/shard_map/psum | solution.py:327
  (312 shorter events, 80.0 us)
Async XLA Ops:
  7.2 157.7 %copy-start = (bf16[1,1024,768]{2,1,0:T(8,128)(2,1)S(1)}, bf16[1,1024,768]{2,1,0:T(8,128)(2,1)}, u32[]{:S(2)}) copy-start(bf16[1,1024,768]{2,1,0:T(8,128)(2,1)} %param.18) | copy-start | bytes 4718596
  7.2 75.2 %all-gather.12.cloned.1.call-start = ((), (), s32[]{:S(2)}) async-start(), calls=%async_computation.10 | async-start | bytes 3981312 | tf_op jit(solution)/shard_map/all_gather | solution.py:271
  7.9 150.8 %all-gather.14.cloned.1.call-start = ((), (), s32[]{:S(2)}) async-start(), calls=%async_computation.11 | async-start | bytes 1327104 | tf_op jit(solution)/shard_map/all_gather | solution.py:273
  8.7 156.2 %all-gather.16.cloned.1.call-start = ((), (), s32[]{:S(2)}) async-start(), calls=%async_computation.12 | async-start | bytes 3981312 | tf_op jit(solution)/shard_map/all_gather | solution.py:274
  9.4 231.4 %all-gather.18.cloned.1.call-start = ((), (), s32[]{:S(2)}) async-start(), calls=%async_computation.13 | async-start | bytes 1327104 | tf_op jit(solution)/shard_map/all_gather | solution.py:276
  10.0 237.6 %all-gather.20.cloned.1.call-start = ((), (), s32[]{:S(2)}) async-start(), calls=%async_computation.14 | async-start | bytes 5308416 | tf_op jit(solution)/shard_map/all_gather | solution.py:277
  10.6 275.0 %all-gather.22.cloned.1.call-start = ((), (), s32[]{:S(2)}) async-start(), calls=%async_computation.15 | async-start | bytes 5308416 | tf_op jit(solution)/shard_map/all_gather | solution.py:279
  11.2 668.3 %reduce-scatter.25.cloned.1.call-start = ((), (), s32[]{:S(2)}) async-start(), calls=%async_computation.18 | async-start | bytes 2654208 | tf_op jit(solution)/shard_map/reduce_scatter | solution.py:318
  12.5 207.0 %copy-start.41 = (pred[1024]{0:T(1024)(128)(4,1)}, pred[1024]{0:T(1024)(128)(4,1)S(1)}, u32[]{:S(2)}) copy-start(pred[1024]{0:T(1024)(128)(4,1)S(1)} %iota_compare_fusion.1) | copy-start | bytes 3076
  58.4 182.4 %copy-start.61 = (f32[768]{0:T(1024)}, f32[768]{0:T(1024)S(1)}, u32[]{:S(2)}) copy-start(f32[768]{0:T(1024)S(1)} %get-tuple-element.223) | copy-start | bytes 9220
  67.8 173.0 %copy-start.75 = (f32[768]{0:T(1024)}, f32[768]{0:T(1024)S(1)}, u32[]{:S(2)}) copy-start(f32[768]{0:T(1024)S(1)} %get-tuple-element.226) | copy-start | bytes 9220
  76.8 59.4 %copy-start.1 = (pred[1024,1024]{0,1:T(8,128)(4,1)}, pred[1024,1024]{0,1:T(8,128)(4,1)S(1)}, u32[]{:S(2)}) copy-start(pred[1024,1024]{0,1:T(8,128)(4,1)S(1)} %fusion.18) | copy-start | bytes 3145732
  82.4 4.5 copy-start.25
  112.3 21.2 %copy-start.26 = (bf16[1,1024,768]{2,1,0:T(8,128)(2,1)S(1)}, bf16[1,1024,768]{2,1,0:T(8,128)(2,1)}, u32[]{:S(2)}) copy-start(bf16[1,1024,768]{2,1,0:T(8,128)(2,1)} %param.17) | copy-start | bytes 4718596
  162.8 78.0 %copy-start.43 = (f32[1024]{0:T(1024)}, f32[1024]{0:T(1024)S(1)}, u32[]{:S(2)}) copy-start(f32[1024]{0:T(1024)S(1)} %broadcast_multiply_fusion.10) | copy-start | bytes 12292
  164.8 76.0 %copy-start.53 = (f32[1024]{0:T(1024)}, f32[1024]{0:T(1024)S(1)}, u32[]{:S(2)}) copy-start(f32[1024]{0:T(1024)S(1)} %add_rsqrt_fusion.2) | copy-start | bytes 12292
  167.7 4.7 copy-start.13
  194.8 22.0 %copy-start.78 = (f32[768]{0:T(1024)S(1)}, f32[768]{0:T(1024)}, u32[]{:S(2)}) copy-start(f32[768]{0:T(1024)} %get-tuple-element.228) | copy-start | bytes 9220
  220.7 20.1 %copy-start.77 = (f32[768]{0:T(1024)S(1)}, f32[768]{0:T(1024)}, u32[]{:S(2)}) copy-start(f32[768]{0:T(1024)} %get-tuple-element.227) | copy-start | bytes 9220
  245.6 87.0 %copy-start.46 = (f32[1024]{0:T(1024)}, f32[1024]{0:T(1024)S(1)}, u32[]{:S(2)}) copy-start(f32[1024]{0:T(1024)S(1)} %broadcast_multiply_fusion.9) | copy-start | bytes 12292
  247.6 85.0 %copy-start.56 = (f32[1024]{0:T(1024)}, f32[1024]{0:T(1024)S(1)}, u32[]{:S(2)}) copy-start(f32[1024]{0:T(1024)S(1)} %add_rsqrt_fusion.1) | copy-start | bytes 12292
  247.7 37.9 %copy-start.72 = (f32[768]{0:T(1024)S(1)}, f32[768]{0:T(1024)}, u32[]{:S(2)}) copy-start(f32[768]{0:T(1024)} %convert_element_type.419) | copy-start | bytes 9220
  321.1 11.5 copy-start.10
  332.6 3.4 copy-start.86
  338.8 5.0 copy-start.31
  338.8 5.0 copy-start.36
  338.8 5.0 copy-start.42
  338.9 342.4 %reduce-scatter.21.cloned.1.call-start = ((), (), s32[]{:S(2)}) async-start(), calls=%async_computation.16 | async-start | bytes 2654208 | tf_op jit(solution)/shard_map/reduce_scatter | solution.py:315
  378.9 40.4 %copy-start.14 = (bf16[1024,768]{0,1:T(8,128)(2,1)S(1)}, bf16[1024,768]{0,1:T(8,128)(2,1)}, u32[]{:S(2)}) copy-start(bf16[1024,768]{0,1:T(8,128)(2,1)} %copy-done.13) | copy-start | bytes 4718596
  419.3 13.5 %copy-start.7 = (f32[1024,768]{0,1:T(8,128)S(1)}, f32[1024,768]{0,1:T(8,128)}, u32[]{:S(2)}) copy-start(f32[1024,768]{0,1:T(8,128)} %copy-done.5) | copy-start | bytes 9437188
  419.3 13.5 %copy-start.19 = (f32[1024,768]{0,1:T(8,128)S(1)}, f32[1024,768]{0,1:T(8,128)}, u32[]{:S(2)}) copy-start(f32[1024,768]{0,1:T(8,128)} %copy-done.18) | copy-start | bytes 9437188
  419.3 13.5 %copy-start.44 = (f32[1024]{0:T(1024)S(1)}, f32[1024]{0:T(1024)}, u32[]{:S(2)}) copy-start(f32[1024]{0:T(1024)} %copy-done.43) | copy-start | bytes 12292
  419.4 13.5 %copy-start.54 = (f32[1024]{0:T(1024)S(1)}, f32[1024]{0:T(1024)}, u32[]{:S(2)}) copy-start(f32[1024]{0:T(1024)} %copy-done.53) | copy-start | bytes 12292
  419.4 13.5 %copy-start.62 = (f32[768]{0:T(1024)S(1)}, f32[768]{0:T(1024)}, u32[]{:S(2)}) copy-start(f32[768]{0:T(1024)} %copy-done.61) | copy-start | bytes 9220
  432.8 4.8 copy-start.32
  439.4 23.1 %copy-start.11 = (f32[1024,768]{0,1:T(8,128)}, f32[1024,768]{0,1:T(8,128)S(1)}, u32[]{:S(2)}) copy-start(f32[1024,768]{0,1:T(8,128)S(1)} %get-tuple-element.252) | copy-start | bytes 9437188
  440.8 21.7 %copy-start.35 = (bf16[1024,768]{0,1:T(8,128)(2,1)}, bf16[1024,768]{0,1:T(8,128)(2,1)S(1)}, u32[]{:S(2)}) copy-start(bf16[1024,768]{0,1:T(8,128)(2,1)S(1)} %convolution_convert_fusion.1) | copy-start | bytes 4718596
  441.4 21.1 %copy-start.85 = (bf16[12,1024,64]{1,2,0:T(8,128)(2,1)S(1)}, bf16[12,1024,64]{1,2,0:T(8,128)(2,1)}, u32[]{:S(2)}) copy-start(bf16[12,1024,64]{1,2,0:T(8,128)(2,1)} %fusion.36) | copy-start | bytes 4718596
  498.9 184.0 %reduce-scatter.31.cloned.1.call-start = ((), (), s32[]{:S(2)}) async-start(), calls=%async_computation.21 | async-start | bytes 7962624
  541.9 13.4 %copy-start.27 = (bf16[1,1024,768]{2,1,0:T(8,128)(2,1)S(1)}, bf16[1,1024,768]{2,1,0:T(8,128)(2,1)}, u32[]{:S(2)}) copy-start(bf16[1,1024,768]{2,1,0:T(8,128)(2,1)} %param.17) | copy-start | bytes 4718596
  541.9 13.4 %copy-start.80 = (bf16[12,1024,64]{1,2,0:T(8,128)(2,1)S(1)}, bf16[12,1024,64]{1,2,0:T(8,128)(2,1)}, u32[]{:S(2)}) copy-start(bf16[12,1024,64]{1,2,0:T(8,128)(2,1)} %get-tuple-element.276) | copy-start | bytes 4718596
  574.6 3.4 copy-start.23
  574.6 3.4 copy-start.24
  600.2 135.4 %reduce-scatter.23.cloned.1.call-start = ((), (), s32[]{:S(2)}) async-start(), calls=%async_computation.17 | async-start | bytes 7962624 | tf_op jit(solution)/shard_map/reduce_scatter | solution.py:316
  641.6 3.1 copy-start.55
  641.7 3.1 copy-start.63
  641.7 3.1 copy-start.76
  649.8 165.8 %reduce-scatter.27.cloned.1.call-start = ((), (), s32[]{:S(2)}) async-start(), calls=%async_computation.19 | async-start | bytes 10616832 | tf_op jit(solution)/shard_map/reduce_scatter | solution.py:319
  661.4 234.1 %reduce-scatter.29.cloned.1.call-start = ((), (), s32[]{:S(2)}) async-start(), calls=%async_computation.20 | async-start | bytes 10616832 | tf_op jit(solution)/shard_map/reduce_scatter | solution.py:321
  673.2 4.0 copy-start.52
  673.2 5.0 copy-start.67
  673.2 271.0 %reduce-scatter.39.cloned.1.call-start = ((), (), s32[]{:S(2)}) async-start(), calls=%async_computation.25 | async-start | bytes 442368
  675.9 293.3 %reduce-scatter.37.cloned.1.call-start = ((), (), s32[]{:S(2)}) async-start(), calls=%async_computation.24 | async-start | bytes 442368
  677.1 328.8 %reduce-scatter.35.cloned.1.call-start = ((), (), s32[]{:S(2)}) async-start(), calls=%async_computation.23 | async-start | bytes 442368
  678.4 364.3 %reduce-scatter.33.cloned.1.call-start = ((), (), s32[]{:S(2)}) async-start(), calls=%async_computation.22 | async-start | bytes 442368
  679.4 469.5 %all-reduce.8.cloned.1.call-start = ((), (), s32[]{:S(2)}) async-start(), calls=%async_computation.26 | async-start | bytes 5013504 | tf_op jit(solution)/shard_map/psum | solution.py:327
  737.6 161.3 %copy-start.15 = (bf16[1,1024,768]{1,2,0:T(8,128)(2,1)S(1)}, bf16[1,1024,768]{1,2,0:T(8,128)(2,1)}, u32[]{:S(2)}) copy-start(bf16[1,1024,768]{1,2,0:T(8,128)(2,1)} %get-tuple-element.255) | copy-start | bytes 4718596
  900.6 3.3 copy-start.40
  900.6 3.3 copy-start.83
  909.4 3.7 copy-start.58
  909.4 3.7 copy-start.66
  909.4 27.4 %copy-start.84 = (bf16[12,1024,64]{1,2,0:T(8,128)(2,1)S(1)}, bf16[12,1024,64]{1,2,0:T(8,128)(2,1)}, u32[]{:S(2)}) copy-start(bf16[12,1024,64]{1,2,0:T(8,128)(2,1)} %convolution_convert_fusion.4) | copy-start | bytes 4718596
  1148.9 7.6 copy-start.39
  1149.0 8.7 copy-start.38
  (40 other events, 77.0 us)
Sparse Core Ops, SparseCore 0:
  9.9 36.7 all-gather.11
  48.6 24.0 all-gather.13
  74.6 33.9 all-gather.15
  110.4 24.0 all-gather.17
  136.2 38.9 all-gather.19
  176.9 38.9 all-gather.21
  338.9 43.2 reduce-scatter.24
  499.0 43.1 reduce-scatter.20
  600.3 65.9 reduce-scatter.30
  670.1 65.4 reduce-scatter.22
  739.2 76.4 reduce-scatter.26
  819.0 76.4 reduce-scatter.28
  898.6 33.8 reduce-scatter.38
  935.3 33.8 reduce-scatter.36
  972.1 33.7 reduce-scatter.34
  1008.9 33.7 reduce-scatter.32
  1046.6 102.3 all-reduce.7
where the time goes:
time: 1180 us; the launch traced here: 1170 us
  matrix products  429 us (36%)
  waiting for transfers between devices  395 us (33%)
  other arithmetic  168 us (14%)
  blocking collectives  92.4 us (8%)
  local copies, waits for them, and re-layouts  61.6 us (5%)
  between operations  18.7 us (2%)
    unnamed x22, waiting for transfers between devices  99.8 us
    psum x1, waiting for transfers between devices, shards(): lax.psum(reduced[0].astype(jnp.bfloat16), 'dp').astype(jnp.float32)  90 us
    convert_element_type x2, other arithmetic, attend_backward(): (probs * (d_probs - jnp.sum(probs * d_probs, axis=-1, keepdims=True))).as...  83.3 us
    reduce_scatter x1, waiting for transfers between devices, shards(): lax.psum_scatter(totals[6], 'fsdp', scatter_dimension=0, tiled=True)  78 us
    dot_general x10, matrix products, matmul(): return jnp.dot(left, right, preferred_element_type=jnp.float32)  77.7 us
    reduce_scatter x1, waiting for transfers between devices, shards(): lax.psum_scatter(totals[8], 'fsdp', scatter_dimension=0, tiled=True)  77.7 us
    dot_general x2, matrix products, attend_backward(): jnp.einsum('hqd,hkd->hqk', d_mixed, head_v, preferred_element_type=jnp.fl...  68.6 us
    unnamed x201, local copies, waits for them, and re-layouts  61.3 us
  transfers between devices with their start and end apart: 17, of which 7 were waited for; matrix products, arithmetic and copies ran while one was open for 50% of the time, Pallas kernels for 0%

commit v1 on v0

v1 whole, which is shorter than its diff:
```python
import jax
import jax.numpy as jnp
from jax import lax
from jax.experimental import pallas as pl
from jax.experimental.pallas import tpu as pltpu
from jax.sharding import PartitionSpec as P

HDIM = 64
PAIR = 2 * HDIM
BLOCK = 256
ROWS = 256
MASKED = -1e30
FACTOR = HDIM ** (-0.5)
BF = jnp.bfloat16
F32 = jnp.float32


def dot_nn(a, b):
    return lax.dot_general(a, b, (((1,), (0,)), ((), ())), preferred_element_type=F32)


def dot_nt(a, b):
    return lax.dot_general(a, b, (((1,), (1,)), ((), ())), preferred_element_type=F32)


def dot_tn(a, b):
    return lax.dot_general(a, b, (((0,), (0,)), ((), ())), preferred_element_type=F32)


def column_sum(values):
    return jnp.sum(values.astype(F32), axis=0, keepdims=True)


def head_lanes(head):
    lane = lax.broadcasted_iota(jnp.int32, (1, PAIR), 1)
    return (lane // HDIM) == head, lane == (HDIM if head == 0 else 0)


def pick(mask, yes, no, shape):
    return jnp.where(jnp.broadcast_to(mask, shape), yes, no)


def length_bias(count, limit):
    positions = lax.broadcasted_iota(jnp.int32, (count, PAIR), 0)
    return jnp.where(positions < limit, 0.0, MASKED).astype(F32)


def causal_edge(values, fill):
    key_at = lax.broadcasted_iota(jnp.int32, values.shape, 0)
    query_at = lax.broadcasted_iota(jnp.int32, values.shape, 1)
    return jnp.where(key_at <= query_at, values, fill)


def attend_forward_kernel(causal, limit_ref, q_ref, k_ref, v_ref, o_ref, lse_ref):
    count, sources = q_ref.shape[0], k_ref.shape[0]
    k_all, v_all = k_ref[...].astype(F32), v_ref[...].astype(F32)
    bias = length_bias(sources, limit_ref[0])
    keys, values = [], []
    for head in range(2):
        own, spare = head_lanes(head)
        keys.append(pick(spare, bias, k_all, k_all.shape).astype(BF))
        ones = pick(spare, 1.0, 0.0, v_all.shape)
        values.append(pick(own, v_all, ones, v_all.shape).T.astype(BF))

    def scores_of(unit):
        block, head = unit
        rows = slice(block * BLOCK, (block + 1) * BLOCK)
        extent = (block + 1) * BLOCK if causal else sources
        own, spare = head_lanes(head)
        q_block = q_ref[rows, :].astype(F32)
        ones = pick(spare, 1.0, 0.0, q_block.shape)
        scores = dot_nt(keys[head][:extent], pick(own, q_block, ones, q_block.shape).astype(BF))
        if causal:
            edge = causal_edge(scores[extent - BLOCK:], MASKED)
            scores = edge if extent == BLOCK else jnp.concatenate([scores[: extent - BLOCK], edge], axis=0)
        return scores

    parts = {}

    def finish(unit, expo, highest):
        block, head = unit
        rows = slice(block * BLOCK, (block + 1) * BLOCK)
        mixed = dot_nn(values[head][:, : expo.shape[0]], expo)
        at = HDIM if head == 0 else 0
        total = mixed[at:at + 1]
        lse_ref[0, head:head + 1, rows] = highest + jnp.log(total)
        parts[unit] = mixed[head * HDIM:(head + 1) * HDIM] * (1.0 / total)
        if head == 1:
            o_ref[rows, :] = jnp.concatenate([parts[(block, 0)], parts[unit]], axis=0).T.astype(BF)

    units = [(block, head) for block in range(count // BLOCK) for head in range(2)]
    ahead = [scores_of(unit) for unit in units[:2]]
    before = None
    for at, unit in enumerate(units):
        if at + 2 < len(units):
            ahead.append(scores_of(units[at + 2]))
        highest = jnp.max(ahead[at], axis=0, keepdims=True)
        expo = jnp.exp(ahead[at] - highest).astype(BF)
        if before is not None:
            finish(*before)
        before = (unit, expo, highest)
    finish(*before)


def attend_backward_kernel(
    causal, limit_ref, q_ref, k_ref, v_ref, o_ref, do_ref, lse_ref, dq_ref, dk_ref, dv_ref, sums_ref, dq_acc
):
    count, sources = q_ref.shape[0], k_ref.shape[0]
    q_all, k_all = q_ref[...].astype(F32), k_ref[...].astype(F32)
    do_all = do_ref[...].astype(F32)
    bias = length_bias(sources, limit_ref[0])
    product = (do_all * o_ref[...].astype(F32)).T
    q_aug, q_own, k_aug, kt_own, do_own, delta, lse = [], [], [], [], [], [], []
    for head in range(2):
        own, spare = head_lanes(head)
        q_aug.append(pick(own, q_all, pick(spare, 1.0, 0.0, q_all.shape), q_all.shape).astype(BF))
        q_own.append(pick(own, q_all, 0.0, q_all.shape).astype(BF))
        k_aug.append(pick(spare, bias, k_all, k_all.shape).astype(BF))
        kt_own.append(pick(own, k_all, 0.0, k_all.shape).T.astype(BF))
        do_own.append(pick(own, do_all, 0.0, do_all.shape).astype(BF))
        delta.append(jnp.sum(product[head * HDIM:(head + 1) * HDIM], axis=0, keepdims=True))
        lse.append(lse_ref[0, head:head + 1, :])

    def products(unit):
        block, head = unit
        rows = slice(block * BLOCK, (block + 1) * BLOCK)
        first = block * BLOCK if causal else 0
        return (
            dot_nt(k_aug[head][rows], q_aug[head][first:]),
            dot_nt(v_ref[rows, :], do_own[head][first:]),
        )

    def gradients(unit, scores, d_probs):
        block, head = unit
        first = block * BLOCK if causal else 0
        probs = jnp.exp(scores - lse[head][:, first:])
        if causal:
            edge = causal_edge(probs[:, :BLOCK], 0.0)
            probs = edge if first + BLOCK == count else jnp.concatenate([edge, probs[:, BLOCK:]], axis=1)
        d_scores = (probs * (d_probs - delta[head][:, first:])).astype(BF)
        return probs.astype(BF), d_scores

    held = {}

    def finish(unit, probs, d_scores):
        block, head = unit
        rows = slice(block * BLOCK, (block + 1) * BLOCK)
        first = block * BLOCK if causal else 0
        dv = dot_nn(probs, do_own[head][first:])
        dk = dot_nn(d_scores, q_own[head][first:])
        dq = dot_nn(kt_own[head][:, rows], d_scores)
        if head == 0:
            held[block] = (dv, dk, dq)
            return
        dv = (held[block][0] + dv).astype(BF)
        dv_ref[rows, :] = dv
        held["dv"] = held.get("dv", 0.0) + column_sum(dv)
        dk_ref[rows, :] = (held[block][1] + dk).astype(BF)
        if block == 0:
            dq_acc[...] = held[block][2] + dq
        else:
            dq_acc[:, first:] += held[block][2] + dq

    units = [(block, head) for block in range(sources // BLOCK) for head in range(2)]
    ahead = [products(units[0])]
    before = None
    for at, unit in enumerate(units):
        if at + 1 < len(units):
            ahead.append(products(units[at + 1]))
        current = (unit,) + gradients(unit, *ahead[at])
        if before is not None:
            finish(*before)
        before = current
    finish(*before)
    dq = dq_acc[...].T.astype(BF)
    dq_ref[...] = dq
    sums_ref[...] = jnp.concatenate([column_sum(dq) * FACTOR, held["dv"], jnp.zeros((6, PAIR), F32)], axis=0)


def attend_forward(q, k, v, limit, causal):
    count, width = q.shape
    sources = k.shape[0]
    pairs = width // PAIR
    of_q = pl.BlockSpec((count, PAIR), lambda i: (0, i))
    of_k = pl.BlockSpec((sources, PAIR), lambda i: (0, i))
    work = 16 * count * sources * width * (5 if causal else 8) // 8
    return pl.pallas_call(
        lambda *refs: attend_forward_kernel(causal, *refs),
        grid=(pairs,),
        in_specs=[pl.BlockSpec(memory_space=pltpu.SMEM), of_q, of_k, of_k],
        out_specs=[of_q, pl.BlockSpec((1, 2, count), lambda i: (i, 0, 0))],
        out_shape=[
            jax.ShapeDtypeStruct((count, width), BF),
            jax.ShapeDtypeStruct((pairs, 2, count), F32),
        ],
        compiler_params=pltpu.CompilerParams(vmem_limit_bytes=40 << 20),
        cost_estimate=pl.CostEstimate(flops=work, bytes_accessed=8 * count * width, transcendentals=0),
        name="attend_forward",
    )(limit, q, k, v)


def attend_backward(q, k, v, o, do, lse, limit, causal):
    count, width = q.shape
    sources = k.shape[0]
    pairs = width // PAIR
    of_q = pl.BlockSpec((count, PAIR), lambda i: (0, i))
    of_k = pl.BlockSpec((sources, PAIR), lambda i: (0, i))
    work = 40 * count * sources * width * (5 if causal else 8) // 8
    return pl.pallas_call(
        lambda *refs: attend_backward_kernel(causal, *refs),
        grid=(pairs,),
        in_specs=[
            pl.BlockSpec(memory_space=pltpu.SMEM),
            of_q,
            of_k,
            of_k,
            of_q,
            of_q,
            pl.BlockSpec((1, 2, count), lambda i: (i, 0, 0)),
        ],
        out_specs=[of_q, of_k, of_k, pl.BlockSpec((8, PAIR), lambda i: (0, i))],
        out_shape=[
            jax.ShapeDtypeStruct((count, width), BF),
            jax.ShapeDtypeStruct((sources, width), BF),
            jax.ShapeDtypeStruct((sources, width), BF),
            jax.ShapeDtypeStruct((8, width), F32),
        ],
        scratch_shapes=[pltpu.VMEM((PAIR, count), F32)],
        compiler_params=pltpu.CompilerParams(vmem_limit_bytes=40 << 20),
        cost_estimate=pl.CostEstimate(flops=work, bytes_accessed=16 * count * width, transcendentals=0),
        name="attend_backward",
    )(limit, q, k, v, o, do, lse)


WHOLE = pl.BlockSpec(memory_space=pltpu.VMEM)
ANYWHERE = pl.BlockSpec(memory_space=pl.ANY)
SCALAR = pl.BlockSpec(memory_space=pltpu.SMEM)
SLAB = 16


def params(limit=48):
    return pltpu.CompilerParams(vmem_limit_bytes=limit << 20)


def cost(flops, *arrays):
    size = sum(a.size * a.dtype.itemsize for a in arrays)
    return pl.CostEstimate(flops=flops, bytes_accessed=size, transcendentals=0)


def of(*shape, dtype=BF):
    return jax.ShapeDtypeStruct(shape, dtype)


def matrix(bundle, index):
    owners, width = bundle.shape[0], bundle.shape[2]
    part = width // owners
    return bundle[:, index * part:(index + 1) * part, :].reshape(width, width)


def fetch(me, pieces, bundle, sem, first):
    copies = []
    for at, ((relative, offset, rows), piece) in enumerate(pieces):
        owner = jnp.bitwise_xor(me, relative)
        if len(bundle.shape) == 3:
            target = bundle.at[owner, pl.ds(offset, rows)]
        else:
            target = bundle.at[pl.ds(pl.multiple_of(owner * rows, 16), rows)]
        copies.append(pltpu.make_async_copy(piece, target, sem.at[first + at]))
        copies[-1].start()
    return copies


def wait_all(copies):
    for copy in copies:
        copy.wait()


def at_first(action):
    pl.when(pl.program_id(0) == 0)(action)


def normalise(summed):
    centred = summed - jnp.mean(summed, axis=-1, keepdims=True)
    inverse = lax.rsqrt(jnp.mean(centred * centred, axis=-1, keepdims=True) + 1e-05)
    return centred * inverse, inverse


def norm_backward(d_out, normed, inverse, gain):
    d_normed = d_out * gain
    return inverse * (
        d_normed
        - jnp.mean(d_normed, axis=-1, keepdims=True)
        - normed * jnp.mean(d_normed * normed, axis=-1, keepdims=True)
    )


def gelu_parts(a):
    bell = jnp.exp(-0.5 * a * a)
    t = 1.0 / (1.0 + 0.23164189 * jnp.abs(a))
    tail = t * (0.127414796 + t * (-0.142248368 + t * (0.7107068705 + t * (-0.7265760135 + t * 0.5307027145)))) * bell
    phi = jnp.where(a >= 0.0, 1.0 - tail, tail)
    return a * phi, phi + a * bell * 0.3989422804014327


def add_rows(ref, rows):
    block = jnp.concatenate(rows + [jnp.zeros((ref.shape[0] - len(rows), ref.shape[1]), F32)], axis=0)

    @pl.when(pl.program_id(0) == 0)
    def _():
        ref[...] = block

    @pl.when(pl.program_id(0) > 0)
    def _():
        ref[...] += block


def pack_kernel(counts, *refs):
    matrices, vectors, out, hold = refs[:counts], refs[counts:-2], refs[-2], refs[-1]
    at = 0
    for ref in matrices:
        out[at:at + ref.shape[0], :] = ref[...]
        at += ref.shape[0]
    hold[...] = jnp.zeros(hold.shape, F32)
    row = 0
    for ref in vectors:
        hold[row:row + ref.shape[0], : ref.shape[1]] = ref[...].astype(F32)
        row += ref.shape[0]
    out[at:, :] = hold[...].astype(BF)


def pack(matrices, vectors, name):
    width = matrices[0].shape[1]
    rows = sum(m.shape[0] for m in matrices) + SLAB
    return pl.pallas_call(
        lambda *refs: pack_kernel(len(matrices), *refs),
        in_specs=[WHOLE] * (len(matrices) + len(vectors)),
        out_specs=WHOLE,
        out_shape=of(rows, width),
        scratch_shapes=[pltpu.VMEM((SLAB, width), F32)],
        compiler_params=params(),
        name=name,
    )(*matrices, *vectors)


def project_kernel(layout, me_ref, x, *refs):
    pieces, (w, vec, q_ref, k_ref, v_ref, sem) = refs[: len(layout)], refs[len(layout):]
    owners, width = w.shape[0], w.shape[2]
    part = width // owners

    @at_first
    def _():
        wait_all(fetch(me_ref[0], list(zip(layout, pieces)), w, sem, 0))
        vec[...] = jnp.zeros(vec.shape, F32)
        for owner in range(owners):
            slab = w[owner, 3 * part:, :].astype(F32)
            vec[:12, owner * part:(owner + 1) * part] = slab[:12, :part]
            for row in range(4):
                at = (owner * 4 + row) * part
                vec[12 + at // width:13 + at // width, at % width:at % width + part] = slab[12 + row:13 + row, :part]

    values = x[...]
    q_ref[...] = ((dot_nn(values, matrix(w, 0)) + vec[0:1, :]) * FACTOR).astype(BF)
    k_ref[...] = dot_nn(values, matrix(w, 1)).astype(BF)
    v_ref[...] = (dot_nn(values, matrix(w, 2)) + vec[1:2, :]).astype(BF)


def project(me, x, pieces, owners):
    count, width = x.shape
    rows = pl.BlockSpec((ROWS, width), lambda i: (i, 0))
    layout = [key for key, _ in pieces]
    return pl.pallas_call(
        lambda *refs: project_kernel(layout, *refs),
        grid=(count // ROWS,),
        in_specs=[SCALAR, rows] + [ANYWHERE] * len(pieces),
        out_specs=[WHOLE, WHOLE, rows, rows, rows],
        out_shape=[of(owners, 3 * width // owners + SLAB, width), of(16, width, dtype=F32)] + [of(count, width)] * 3,
        scratch_shapes=[pltpu.SemaphoreType.DMA((len(pieces),))],
        compiler_params=params(),
        cost_estimate=cost(6 * count * width * width, x, x, x, x, x),
        name="self_project",
    )(me, x, *[piece for _, piece in pieces])


def between_kernel(layouts, me_ref, vec, o, x, mem, *refs):
    count = len(layouts[0])
    ones, twos = refs[:count], refs[count:count + len(layouts[1])]
    w, wo, z_ref, r_ref, h_ref, q_ref, k_ref, v_ref, sem = refs[count + len(layouts[1]):]

    @at_first
    def _():
        copies = fetch(me_ref[0], list(zip(layouts[0], ones)), w, sem, 0)
        copies += fetch(me_ref[0], list(zip(layouts[1], twos)), wo, sem, count)
        wait_all(copies)

    summed = x[...].astype(F32) + dot_nn(o[...], matrix(wo, 0)) + vec[2:3, :]
    source = mem[...]
    k_ref[...] = dot_nn(source, matrix(w, 1)).astype(BF)
    v_ref[...] = (dot_nn(source, matrix(w, 2)) + vec[4:5, :]).astype(BF)
    z, r = normalise(summed)
    z_ref[...] = z
    r_ref[...] = r
    hidden = (z * vec[6:7, :] + vec[9:10, :]).astype(BF)
    h_ref[...] = hidden
    q_ref[...] = ((dot_nn(hidden, matrix(w, 0)) + vec[3:4, :]) * FACTOR).astype(BF)


def between(me, vec, o, x, mem, ones, twos, owners):
    count, width = x.shape
    part = width // owners
    rows = pl.BlockSpec((ROWS, width), lambda i: (i, 0))
    layouts = [key for key, _ in ones], [key for key, _ in twos]
    return pl.pallas_call(
        lambda *refs: between_kernel(layouts, *refs),
        grid=(count // ROWS,),
        in_specs=[SCALAR, WHOLE, rows, rows, rows] + [ANYWHERE] * (len(ones) + len(twos)),
        out_specs=[WHOLE, WHOLE, rows, pl.BlockSpec((ROWS, 1), lambda i: (i, 0))] + [rows] * 4,
        out_shape=[
            of(owners, 3 * part, width), of(owners, 2 * part + SLAB, width), of(count, width, dtype=F32),
            of(count, 1, dtype=F32),
        ] + [of(count, width)] * 4,
        scratch_shapes=[pltpu.SemaphoreType.DMA((len(ones) + len(twos),))],
        compiler_params=params(),
        cost_estimate=cost(8 * count * width * width, x, x, x, x, x, x, x, x, x),
        name="self_out_cross_project",
    )(me, vec, o, x, mem, *[piece for _, piece in ones + twos])


def ffn_kernel(layouts, me_ref, vec, o, z_in, cot, wo, *refs):
    count = len(layouts[0])
    ins, outs = refs[:count], refs[count:count + len(layouts[1])]
    (mixed, act_ref, da_ref, df_ref, h_ref, dy_ref, db_ref, do_ref, sums_ref, w_in, w_out, slope, b_out, sem) = (
        refs[count + len(layouts[1]):]
    )
    width = o.shape[1]
    chunks = w_in.shape[1] // width
    owners = wo.shape[0]
    part = width // owners
    in_copies = list(zip(layouts[0], ins)), list(zip(layouts[1], outs))

    @at_first
    def _():
        copies = fetch(me_ref[0], in_copies[0], w_in, sem, 0) + fetch(me_ref[0], in_copies[1], w_out, sem, count)
        for owner in range(owners):
            b_out[0:1, owner * part:(owner + 1) * part] = wo[owner, 2 * part:, :].astype(F32)[0:1, :part]
        wait_all(copies)

    gains = [vec[6 + i:7 + i, :] for i in range(3)]
    shifts = [vec[9 + i:10 + i, :] for i in range(3)]
    first = z_in[...] * gains[0] + shifts[0]
    z_two, r_two = normalise(first + dot_nn(o[...], matrix(wo, 1)) + vec[5:6, :])
    second = z_two * gains[1] + shifts[1]
    hidden = second.astype(BF)
    h_ref[...] = hidden

    def columns(c):
        return slice(c * width, (c + 1) * width)

    total = second + b_out[0:1, :]
    ahead = dot_nn(hidden, w_in[:, columns(0)])
    before = None
    for c in range(chunks):
        pre = ahead + vec[12 + c:13 + c, :]
        if c + 1 < chunks:
            ahead = dot_nn(hidden, w_in[:, columns(c + 1)])
        act, grad = gelu_parts(pre)
        act = act.astype(BF)
        act_ref[:, columns(c)] = act
        slope[:, columns(c)] = grad
        if before is not None:
            total = total + dot_nn(before, w_out[columns(c - 1), :])
        before = act
    total = total + dot_nn(before, w_out[columns(chunks - 1), :])
    z, r = normalise(total)
    mixed[...] = (z * gains[2] + shifts[2]).astype(BF)
    incoming = cot[...].astype(F32)
    dy_three = norm_backward(incoming, z, r, gains[2])
    df = dy_three.astype(BF)
    df_ref[...] = df
    rows = [column_sum(df), column_sum(incoming * z), column_sum(incoming)]

    da_sums = []
    d_two = dy_three
    ahead = dot_nt(df, w_out[columns(0), :])
    before = None
    for c in range(chunks):
        d_act = ahead
        if c + 1 < chunks:
            ahead = dot_nt(df, w_out[columns(c + 1), :])
        da = (d_act * slope[:, columns(c)]).astype(BF)
        da_ref[:, columns(c)] = da
        da_sums.append(column_sum(da))
        if before is not None:
            d_two = d_two + dot_nt(before, w_in[:, columns(c - 1)])
        before = da
    d_two = d_two + dot_nt(before, w_in[:, columns(chunks - 1)])
    dy_two = norm_backward(d_two, z_two, r_two, gains[1])
    dy_ref[...] = dy_two
    db = dy_two.astype(BF)
    db_ref[...] = db
    do_ref[...] = dot_nt(db, matrix(wo, 1)).astype(BF)
    rows += [column_sum(d_two * z_two), column_sum(d_two), column_sum(db)]
    add_rows(sums_ref, rows + da_sums)


def ffn(me, vec, o, z, cot, wo, ins, outs, hidden):
    count, width = o.shape
    rows = pl.BlockSpec((ROWS, width), lambda i: (i, 0))
    wide = pl.BlockSpec((ROWS, hidden), lambda i: (i, 0))
    layouts = [key for key, _ in ins], [key for key, _ in outs]
    return pl.pallas_call(
        lambda *refs: ffn_kernel(layouts, *refs),
        grid=(count // ROWS,),
        in_specs=[SCALAR, WHOLE, rows, rows, rows, WHOLE] + [ANYWHERE] * (len(ins) + len(outs)),
        out_specs=[rows, wide, wide, rows, rows, rows, rows, rows, pl.BlockSpec((16, width), lambda i: (0, 0))],
        out_shape=[
            of(count, width), of(count, hidden), of(count, hidden), of(count, width), of(count, width),
            of(count, width, dtype=F32), of(count, width), of(count, width), of(16, width, dtype=F32),
        ],
        scratch_shapes=[
            pltpu.VMEM((width, hidden), BF),
            pltpu.VMEM((hidden, width), BF),
            pltpu.VMEM((ROWS, hidden), F32),
            pltpu.VMEM((8, width), F32),
            pltpu.SemaphoreType.DMA((len(ins) + len(outs),)),
        ],
        compiler_params=params(56),
        cost_estimate=cost(8 * count * width * hidden + 4 * count * width * width, o, z, z, cot, o, o, o, o),
        name="ffn",
    )(me, vec, o, z, cot, wo, *[piece for _, piece in ins + outs])


def cross_back_kernel(vec, dq, dy, z, r, w, wo, dy_ref, db_ref, do_ref, sums_ref):
    d_one = dy[...] + dot_nt(dq[...], matrix(w, 0)) * FACTOR
    normed = z[...]
    dy_one = norm_backward(d_one, normed, r[...], vec[6:7, :])
    dy_ref[...] = dy_one
    db = dy_one.astype(BF)
    db_ref[...] = db
    do_ref[...] = dot_nt(db, matrix(wo, 0)).astype(BF)
    add_rows(sums_ref, [column_sum(d_one * normed), column_sum(d_one), column_sum(db)])


def cross_back(vec, dq, dy, z, r, w, wo):
    count, width = dq.shape
    rows = pl.BlockSpec((ROWS, width), lambda i: (i, 0))
    return pl.pallas_call(
        cross_back_kernel,
        grid=(count // ROWS,),
        in_specs=[WHOLE] + [rows] * 3 + [pl.BlockSpec((ROWS, 1), lambda i: (i, 0)), WHOLE, WHOLE],
        out_specs=[rows] * 3 + [pl.BlockSpec((8, width), lambda i: (0, 0))],
        out_shape=[of(count, width, dtype=F32), of(count, width), of(count, width), of(8, width, dtype=F32)],
        compiler_params=params(),
        cost_estimate=cost(4 * count * width * width, dq, dy, z, dy, dq, dq, w, wo),
        name="cross_query_back",
    )(vec, dq, dy, z, r, w, wo)


def memory_back_kernel(dk, dv, w, out):
    out[...] = dot_nt(dk[...], matrix(w, 1)) + dot_nt(dv[...], matrix(w, 2))


def memory_back(dk, dv, w):
    count, width = dk.shape
    rows = pl.BlockSpec((ROWS, width), lambda i: (i, 0))
    return pl.pallas_call(
        memory_back_kernel,
        grid=(count // ROWS,),
        in_specs=[rows, rows, WHOLE],
        out_specs=rows,
        out_shape=of(count, width, dtype=F32),
        compiler_params=params(),
        cost_estimate=cost(4 * count * width * width, dk, dv, dk, dk, w),
        name="memory_back",
    )(dk, dv, w)


def self_back_kernel(dq, dk, dv, dy, w, out):
    total = dy[...] + dot_nt(dq[...], matrix(w, 0)) * FACTOR
    out[...] = total + dot_nt(dk[...], matrix(w, 1)) + dot_nt(dv[...], matrix(w, 2))


def self_back(dq, dk, dv, dy, w):
    count, width = dq.shape
    rows = pl.BlockSpec((ROWS, width), lambda i: (i, 0))
    return pl.pallas_call(
        self_back_kernel,
        grid=(count // ROWS,),
        in_specs=[rows] * 4 + [WHOLE],
        out_specs=rows,
        out_shape=of(count, width, dtype=F32),
        compiler_params=params(),
        cost_estimate=cost(6 * count * width * width, dq, dk, dv, dy, dy, w),
        name="self_project_back",
    )(dq, dk, dv, dy, w)


def weight_grad_kernel(items, slabs, me_ref, *refs):
    ins, (keep, send, hold, extra) = refs[:-4], refs[-4:]
    me = me_ref[0]
    width = hold.shape[2]
    part = width // 8
    for at, (left, right, left_chunk, right_chunk, scale) in enumerate(items):
        a = ins[left][:, left_chunk * width:(left_chunk + 1) * width]
        b = ins[right][:, right_chunk * width:(right_chunk + 1) * width]
        product = dot_tn(a, b)
        hold[at % 2] = product if scale == 1.0 else product * scale
        for relative in range(8):
            owner = jnp.bitwise_xor(me, relative)
            block = hold[at % 2, pl.ds(pl.multiple_of(owner * part, part), part), :].astype(BF)
            (send if relative % 2 else keep)[relative // 2, at * part:(at + 1) * part, :] = block
    if slabs:
        row = 0
        extra[...] = jnp.zeros(extra.shape, F32)
        for ref in ins[len(ins) - slabs:]:
            extra[row:row + ref.shape[0], :] = ref[...]
            row += ref.shape[0]
        block = extra[...].astype(BF)
        for relative in range(8):
            (send if relative % 2 else keep)[relative // 2, part * len(items):, :] = block


def weight_grad(me, operands, items, name, slabs=(), slab_rows=0):
    width = operands[0].shape[1]
    part = width // 8
    shape = of(4, part * len(items) + slab_rows, width)
    return pl.pallas_call(
        lambda *refs: weight_grad_kernel(items, len(slabs), *refs),
        in_specs=[SCALAR] + [WHOLE] * (len(operands) + len(slabs)),
        out_specs=[WHOLE, WHOLE],
        out_shape=[shape, shape],
        scratch_shapes=[pltpu.VMEM((2, width, width), F32), pltpu.VMEM((max(slab_rows, 8), width), F32)],
        compiler_params=params(54),
        cost_estimate=cost(2 * operands[0].shape[0] * width * width * len(items), *operands),
        name=name,
    )(me, *operands, *slabs)


def tall_grad_kernel(me_ref, left, right, keep, send, hold):
    me = me_ref[0]
    width = right.shape[1]
    part = left.shape[1] // 8
    for c in range(left.shape[1] // width):
        hold[c * width:(c + 1) * width, :] = dot_tn(left[:, c * width:(c + 1) * width], right[...]).astype(BF)
    for relative in range(8):
        owner = jnp.bitwise_xor(me, relative)
        block = hold[pl.ds(pl.multiple_of(owner * part, part), part), :]
        (send if relative % 2 else keep)[relative // 2] = block


def tall_grad(me, left, right, name):
    tall, width = left.shape[1], right.shape[1]
    shape = of(4, tall // 8, width)
    return pl.pallas_call(
        tall_grad_kernel,
        in_specs=[SCALAR, WHOLE, WHOLE],
        out_specs=[WHOLE, WHOLE],
        out_shape=[shape, shape],
        scratch_shapes=[pltpu.VMEM((tall, width), BF)],
        compiler_params=params(54),
        cost_estimate=cost(2 * left.shape[0] * tall * width, left, left, right),
        name=name,
    )(me, left, right)


def swap(value, bit, axis="fsdp", size=8):
    return lax.ppermute(value, axis, [(i, i ^ bit) for i in range(size)])


def tie(*values):
    return lax.optimization_barrier(values)


def local(kernel, name, out_shape, *args, scratch=(), scalars=0):
    return pl.pallas_call(
        kernel,
        in_specs=[SCALAR] * scalars + [WHOLE] * (len(args) - scalars),
        out_specs=[WHOLE] * len(out_shape),
        out_shape=out_shape,
        scratch_shapes=scratch,
        compiler_params=params(),
        cost_estimate=cost(0, *args, *out_shape),
        name=name,
    )(*args)


def split_kernel(keep, came, own, to_x, to_y, to_far):
    own[...] = keep[0].astype(F32) + came[0].astype(F32)
    for index, ref in enumerate((to_x, to_y, to_far)):
        ref[...] = (keep[index + 1].astype(F32) + came[index + 1].astype(F32)).astype(BF)


def reduce_core(keep, send):
    return [keep, swap(send, 1)]


def reduce_plane(state):
    keep, came = state
    rows, width = keep.shape[1:]
    own, to_x, to_y, to_far = local(
        split_kernel, "grad_split", [of(rows, width, dtype=F32)] + [of(rows, width)] * 3, keep, came
    )
    return [own, swap(to_far, 6), swap(to_x, 2), swap(to_y, 4)]


def quarter_kernel(at_ref, own, far, from_x, from_y, mine, one, two, three):
    at = at_ref[0]
    rows = mine.shape[0]
    for index, ref in enumerate((mine, one, two, three)):
        place = pl.ds(pl.multiple_of(jnp.bitwise_xor(at, index) * rows, rows), rows)
        total = own[place, :] + far[place, :].astype(F32) + from_x[place, :].astype(F32) + from_y[place, :].astype(F32)
        ref[...] = total.astype(ref.dtype)


def depth_index():
    return lax.axis_index("dp").astype(jnp.int32).reshape(1)


def reduce_quarters(state):
    rows, width = state[0].shape
    shapes = [of(rows // 4, width, dtype=F32)] + [of(rows // 4, width)] * 3
    mine, one, two, three = local(quarter_kernel, "grad_quarters", shapes, depth_index(), *state, scalars=1)
    return [mine, swap(three, 3, "dp", 4), swap(two, 2, "dp", 4), swap(one, 1, "dp", 4)]


def add_kernel(mine, three, two, one, out):
    out[...] = (mine[...] + three[...].astype(F32) + two[...].astype(F32) + one[...].astype(F32)).astype(BF)


def reduce_return(state):
    (mine,) = local(add_kernel, "grad_add", [of(*state[0].shape)], *state)
    return [mine, swap(mine, 3, "dp", 4), swap(mine, 2, "dp", 4), swap(mine, 1, "dp", 4)]


def place_kernel(spans, at_ref, mine, three, two, one, *refs):
    outs, hold = refs[:-1], refs[-1]
    at = at_ref[0]
    rows = mine.shape[0]
    for relative, ref in enumerate((mine, one, two, three)):
        hold[pl.ds(pl.multiple_of(jnp.bitwise_xor(at, relative) * rows, rows), rows), :] = ref[...].astype(F32)
    for (first, count, columns), out in zip(spans, outs):
        if len(out.shape) == 3:
            for index in range(out.shape[0]):
                out[index] = hold[first + index * out.shape[1]:first + (index + 1) * out.shape[1], :]
        else:
            for column in range(columns):
                begin = first + column * count
                out[:, column * hold.shape[1]:(column + 1) * hold.shape[1]] = hold[begin:begin + count, :]


def reduce_end(state, spans, shapes):
    rows, width = state[0].shape
    return local(
        lambda *refs: place_kernel(spans, *refs), "grad_place", shapes, depth_index(), *state,
        scratch=[pltpu.VMEM((4 * rows, width), F32)], scalars=1,
    )


def small_kernel(me_ref, early, late, self_b, cross_b, gain, shift, b_in, b_out):
    me = me_ref[0]
    width, part = early.shape[1], self_b.shape[1]
    turn = lax.rem(width - me * part, width)

    def own(ref, row):
        return pltpu.roll(ref[row // 8 * 8:row // 8 * 8 + 8, :], turn, 1)[row % 8:row % 8 + 1, :part]

    for ref, rows in ((gain, (16, 3, 1)), (shift, (17, 4, 2))):
        for index, row in enumerate(rows):
            ref[index:index + 1, :] = own(early, row)
    b_out[...] = own(early, 0)
    cross_b[0:1, :] = own(early, 24)
    cross_b[1:2, :] = own(early, 25)
    cross_b[2:3, :] = own(early, 5)
    self_b[0:1, :] = own(late, 0)
    self_b[1:2, :] = own(late, 1)
    self_b[2:3, :] = own(early, 18)
    wide = b_in.shape[1]
    row = early[pl.ds(6 + me * wide // width, 1), :]
    b_in[...] = jnp.where(lax.rem(me, 2) == 0, row[:, :wide], row[:, wide:])


def reduce_plain(sizes, blocks):
    value = lax.psum_scatter(blocks.astype(F32), "fsdp", scatter_dimension=0, tiled=False)
    return lax.psum(value.astype(BF), "dp").astype(F32)


def first_hops(shard):
    return swap(shard, 2), swap(shard, 4)


def pieces_of(shard, x, y, far, offsets=(0,)):
    rows = shard.shape[0]
    found = [((0, 0, rows), shard), ((1, 0, rows), swap(shard, 1)), ((2, 0, rows), x), ((4, 0, rows), y)]
    found += [((3, 0, rows), swap(x, 1)), ((5, 0, rows), swap(y, 1))]
    for offset, piece in zip(offsets, far):
        found += [((6, offset, piece.shape[0]), piece), ((7, offset, piece.shape[0]), swap(piece, 1))]
    return found


def shards(sizes, target, memory, target_lengths, memory_lengths, self_qkv, self_bias, self_out, cross_qkv, cross_bias,
           cross_out, ffn_in, ffn_in_bias, ffn_out, ffn_out_bias, norm_gain, norm_bias, cotangent):
    n = sizes[0]
    fast = n == 8 and sizes[1] == 4
    width, hidden = target.shape[-1], ffn_in.shape[1]
    part, wide = width // n, hidden // n
    ratio = hidden // width
    x, mem, cot = target[0], memory[0], cotangent[0]
    place = lax.axis_index("fsdp").astype(jnp.int32)
    me = place.reshape(1)
    vectors = [self_bias, cross_bias, norm_gain, norm_bias, ffn_in_bias.reshape(ratio, part)]

    if fast:
        owners = 8
        own = pack([self_qkv.reshape(3 * part, width)], vectors, "pack_self")
        half = own.shape[0] // 32 * 16
        s_x, s_y = first_hops(own)
        s_low, s_high = swap(s_y[:half], 2), swap(s_x[half:], 4)
        c_one = cross_qkv.reshape(3 * part, width)
        c_two = pack([self_out, cross_out], [ffn_out_bias.reshape(1, part)], "pack_out")
        _, _, c_one, c_two = tie(s_x, s_y, c_one, c_two)
        c_one_x, c_one_y = first_hops(c_one)
        c_two_x, c_two_y = first_hops(c_two)
        self_pieces = pieces_of(own, s_x, s_y, (s_low, s_high), (0, half))
    else:
        owners, me = 1, jnp.zeros((1,), jnp.int32)

        def gathered(member, axis):
            return lax.all_gather(member, "fsdp", axis=axis, tiled=True)

        def single(value):
            return [((0, 0, value.shape[0]), value)]

        fulls = [gathered(member, 1) for member in vectors[:4]] + [gathered(ffn_in_bias, 0).reshape(ratio, width)]
        last = jnp.pad(gathered(ffn_out_bias, 0).reshape(1, width), ((0, SLAB - 1), (0, 0)))
        self_pieces = single(jnp.concatenate([gathered(self_qkv, 1).reshape(3 * width, width)] + fulls))
        ones = single(gathered(cross_qkv, 1).reshape(3 * width, width))
        twos = single(jnp.concatenate([gathered(self_out, 0), gathered(cross_out, 0), last]))
        in_pieces, out_pieces = single(gathered(ffn_in, 0)), single(gathered(ffn_out, 0))

    self_w, vec, q, k, v = project(me, x, self_pieces, owners)
    if fast:
        q, c_one_x, c_one_y, c_two_x, c_two_y, f_in, f_out = tie(q, c_one_x, c_one_y, c_two_x, c_two_y, ffn_in, ffn_out)
        c_one_far, c_two_far = swap(c_one_y, 2), swap(c_two_x, 4)
        f_in_x, f_in_y = first_hops(f_in)
        f_out_x, f_out_y = first_hops(f_out)
    o, lse = attend_forward(q, k, v, target_lengths, True)
    if fast:
        o, c_one_far, c_two_far = tie(o, c_one_far, c_two_far)
        ones = pieces_of(c_one, c_one_x, c_one_y, (c_one_far,))
        twos = pieces_of(c_two, c_two_x, c_two_y, (c_two_far,))
    cross_w, out_w, z_one, r_one, h_one, q2, k2, v2 = between(me, vec, o, x, mem, ones, twos, owners)
    if fast:
        q2, f_in_x, f_in_y, f_out_x, f_out_y = tie(q2, f_in_x, f_in_y, f_out_x, f_out_y)
        f_in_far, f_out_far = swap(f_in_y, 2), swap(f_out_x, 4)
    o2, lse2 = attend_forward(q2, k2, v2, memory_lengths, False)
    if fast:
        o2, f_in_far, f_out_far = tie(o2, f_in_far, f_out_far)
        in_pieces = pieces_of(f_in, f_in_x, f_in_y, (f_in_far,))
        out_pieces = pieces_of(f_out, f_out_x, f_out_y, (f_out_far,))
    mixed, act, da, df, h_two, dy, db2, do2, ffn_sums = ffn(
        me, vec, o2, z_one, cot, out_w, in_pieces, out_pieces, hidden
    )
    if fast:
        out_state = reduce_core(*tall_grad(me, act, df, "ffn_out_grad"))
        h_two, out_state[0] = tie(h_two, out_state[0])
        items = [(0, 1, 0, c, 1.0) for c in range(ratio)]
        in_state = reduce_core(*weight_grad(me, [h_two, da], items, "ffn_in_grad"))
        do2, *out_state = tie(do2, *out_state)
        out_state = reduce_plane(out_state)
        do2, in_state[0], out_state[0] = tie(do2, in_state[0], out_state[0])
    dq2, dk2, dv2, cross_sums = attend_backward(q2, k2, v2, o2, do2, lse2, memory_lengths, False)
    if fast:
        dq2, *states = tie(dq2, *out_state, *in_state)
        out_state, in_state = reduce_quarters(states[:4]), reduce_plane(states[4:])
        dq2, out_state[0], in_state[0] = tie(dq2, out_state[0], in_state[0])
    dy_one, db, do, back_sums = cross_back(vec, dq2, dy, z_one, r_one, cross_w, out_w)
    if fast:
        db, *states = tie(db, *out_state)
        out_state = reduce_return(states)
        operands = [h_one, dq2, mem, dk2, dv2, o2, db2, o, db]
        items = [(0, 1, 0, 0, FACTOR), (2, 3, 0, 0, 1.0), (2, 4, 0, 0, 1.0), (5, 6, 0, 0, 1.0), (7, 8, 0, 0, 1.0)]
        cross_state = reduce_core(
            *weight_grad(me, operands, items, "cross_grad", (ffn_sums, back_sums, cross_sums), 2 * SLAB)
        )
        do, *states = tie(do, *in_state, cross_state[0], out_state[0])
        in_state = reduce_quarters(states[:4])
        do, in_state[0] = tie(do, in_state[0])
    dq, dk, dv, self_sums = attend_backward(q, k, v, o, do, lse, target_lengths, True)
    if fast:
        dq, *states = tie(dq, *in_state, *cross_state)
        in_state, cross_state = reduce_return(states[:4]), reduce_plane(states[4:])
        items = [(0, 1, 0, 0, FACTOR), (0, 2, 0, 0, 1.0), (0, 3, 0, 0, 1.0)]
        self_state = reduce_core(*weight_grad(me, [x, dq, dk, dv], items, "self_grad", (self_sums,), 2 * SLAB))
        dq, dk2, self_state[0], cross_state[0] = tie(dq, dk2, self_state[0], cross_state[0])
    d_target = self_back(dq, dk, dv, dy_one, self_w)
    if fast:
        d_target, dk2, *self_state = tie(d_target, dk2, *self_state)
        self_state = reduce_plane(self_state)
    d_memory = memory_back(dk2, dv2, cross_w)

    if fast:
        f32 = dict(dtype=F32)
        (out_sum,) = reduce_end(out_state, [(0, wide, 1)], [of(wide, width, **f32)])
        (in_sum,) = reduce_end(in_state, [(0, part, ratio)], [of(part, hidden, **f32)])
        cross_state = reduce_quarters(cross_state)
        self_state = reduce_quarters(self_state)
        cross_w_sum, cross_o_sum, self_o_sum, early = reduce_end(
            reduce_return(cross_state),
            [(0, 0, 0), (3 * part, part, 1), (4 * part, part, 1), (5 * part, 2 * SLAB, 1)],
            [of(3, part, width, **f32), of(part, width, **f32), of(part, width, **f32), of(2 * SLAB, width, **f32)],
        )
        self_w_sum, late = reduce_end(
            reduce_return(self_state), [(0, 0, 0), (3 * part, 2 * SLAB, 1)],
            [of(3, part, width, **f32), of(2 * SLAB, width, **f32)],
        )
        shapes = [of(3, part, **f32)] * 4 + [of(1, wide, **f32), of(1, part, **f32)]
        self_b, cross_b, gain, shift, b_in, b_out = local(small_kernel, "small_grads", shapes, me, early, late, scalars=1)
        b_in, b_out = b_in[0], b_out[0]
    else:
        def whole(left, right, scale=1.0):
            return reduce_plain(sizes, (dot_tn(left, right) * scale).reshape(n, left.shape[1] // n, right.shape[1]))

        def mine(rows, size):
            rows = rows.reshape(-1, n * size)
            return lax.dynamic_slice(rows, (0, place * size), (rows.shape[0], size))

        self_w_sum = jnp.stack([whole(x, dq, FACTOR), whole(x, dk), whole(x, dv)])
        cross_w_sum = jnp.stack([whole(h_one, dq2, FACTOR), whole(mem, dk2), whole(mem, dv2)])
        cross_o_sum, self_o_sum = whole(o2, db2), whole(o, db)
        in_sum, out_sum = whole(h_two, da), whole(act, df)
        sums = lax.psum(jnp.concatenate([ffn_sums, back_sums, cross_sums, self_sums]), ("fsdp", "dp"))
        narrow = mine(sums, part)
        self_b = jnp.stack([narrow[32], narrow[33], narrow[18]])
        cross_b = jnp.stack([narrow[24], narrow[25], narrow[5]])
        gain = jnp.stack([narrow[16], narrow[3], narrow[1]])
        shift = jnp.stack([narrow[17], narrow[4], narrow[2]])
        b_in, b_out = mine(sums[6:10], wide)[0], narrow[0]
    return (
        mixed[None], d_target[None], d_memory[None], self_w_sum, self_b, self_o_sum, cross_w_sum, cross_b, cross_o_sum,
        in_sum, b_in, out_sum, b_out, gain, shift,
    )


def solution(mesh):
    rows = P(("fsdp", "dp"), None, None)
    row = P(("fsdp", "dp"))
    stacked, vectors, matrix, vector = P(None, "fsdp", None), P(None, "fsdp"), P("fsdp", None), P("fsdp")
    weights = (stacked, vectors, matrix, stacked, vectors, matrix, matrix, vector, matrix, vector, vectors, vectors)
    sizes = (mesh.shape["fsdp"], mesh.shape["dp"])
    return jax.shard_map(
        lambda *args: shards(sizes, *args),
        mesh=mesh,
        in_specs=(rows, rows, row, row) + weights + (rows,),
        out_specs=(rows, rows, rows) + weights,
        check_vma=False,
    )
```

time: 1180 us -> 508 us (0.43)
  matrix products: 429 us -> 0 us
  waiting for transfers between devices: 395 us -> 142 us
  Pallas kernels: 0 us -> 246 us
  other arithmetic: 168 us -> 0.6 us
  blocking collectives: 92.4 us -> 0 us
  starting transfers between devices: 0.68 us -> 73.8 us
  local copies, waits for them, and re-layouts: 61.6 us -> 33.9 us
  between operations: 18.7 us -> 3 us
    dot_general x42 -> x0, matrix products: 429 us -> none  [the longest x10 77.7 us: matmul(): return jnp.dot(left, right, preferred_element_type=jnp.float32)]
    pallas_call x0 -> x33, Pallas kernels: none -> 246 us  [the longest x2 58.7 us: attend_backward(): pl.pallas_call(lambda *refs: attend_backward_kernel(causal, *refs), grid=...]
    reduce_scatter x5 -> x0, waiting for transfers between devices: 206 us -> none  [the longest x1 78 us: shards(): lax.psum_scatter(totals[6], 'fsdp', scatter_dimension=0, tiled=True)]
    ppermute x0 -> x77, waiting for transfers between devices: none -> 142 us  [swap(): return lax.ppermute(value, axis, [(i, i ^ bit) for i in range(size)])]
    convert_element_type x20 -> x0, other arithmetic: 105 us -> none  [the longest x2 83.3 us: attend_backward(): (probs * (d_probs - jnp.sum(probs * d_probs, axis=-1, keepdims=True))).as...]
    unnamed x22 -> x0, waiting for transfers between devices: 99.8 us -> none
    psum x1 -> x0, waiting for transfers between devices: 90 us -> none  [shards(): lax.psum(reduced[0].astype(jnp.bfloat16), 'dp').astype(jnp.float32)]
    ppermute x0 -> x77, starting transfers between devices: none -> 73.8 us  [swap(): return lax.ppermute(value, axis, [(i, i ^ bit) for i in range(size)])]
  transfers between devices with their start and end apart: 17 -> 77, of which waited for: 7 -> 25; matrix products, arithmetic and copies ran while one was open for 50% -> 0% of each run, Pallas kernels for 0% -> 33%
where the time goes in v1:
time: 508 us; the launch traced here: 499 us
  Pallas kernels  246 us (48%)
  waiting for transfers between devices  142 us (28%)
  starting transfers between devices  73.8 us (15%)
  local copies, waits for them, and re-layouts  33.9 us (7%)
    ppermute x77, waiting for transfers between devices, swap(): return lax.ppermute(value, axis, [(i, i ^ bit) for i in range(size)])  142 us
    ppermute x77, starting transfers between devices, swap(): return lax.ppermute(value, axis, [(i, i ^ bit) for i in range(size)])  73.8 us
    pallas_call x2, Pallas kernels, attend_backward(): pl.pallas_call(lambda *refs: attend_backward_kernel(causal, *refs), grid=...  58.7 us
    pallas_call x1, Pallas kernels, ffn(): pl.pallas_call(lambda *refs: ffn_kernel(layouts, *refs), grid=(count // R...  46 us
    pallas_call x3, Pallas kernels, weight_grad(): pl.pallas_call(lambda *refs: weight_grad_kernel(items, len(slabs), *refs)...  34.5 us
    unnamed x136, local copies, waits for them, and re-layouts  33.1 us
    pallas_call x2, Pallas kernels, attend_forward(): pl.pallas_call(lambda *refs: attend_forward_kernel(causal, *refs), grid=(...  32.2 us
    pallas_call x17, Pallas kernels, local(): pl.pallas_call(kernel, in_specs=[SCALAR] * scalars + [WHOLE] * (len(args)...  16.8 us
  transfers between devices with their start and end apart: 77, of which 25 were waited for; matrix products, arithmetic and copies ran while one was open for 0% of the time, Pallas kernels for 33%

profile of v1, /device:TPU:0, one launch (start us, length us, event | category | flops | bytes accessed | tf_op | source)
XLA Modules:
  0.0 498.9 jit_solution(11823275198335981704)
XLA Ops:
  5.2 3.0 collective-permute-start.2
  8.2 1.5 collective-permute-start.1
  9.7 9.2 %collective-permute-done.2.refs_5_ = bf16[304,768]{1,0:T(8,128)(2,1)S(1)} collective-permute-done((bf16[304,768]{1,0:T(8,128)(2,1)S(1)}, bf16[304,768]{1,0:T(8,128)(2,1)S(1)}, u32[]{:S(2)}, u32[]{:S(2)}) %collective-permute-start.2) | collective-permute-done | bytes 466976 | tf_op jit(solution)/shard_map/ppermute | solution.py:666
  18.9 1.8 collective-permute-start.5
  20.8 1.6 collective-permute-start.7
  22.8 2.8 collective-permute-done.5.refs_8_
  25.6 1.7 collective-permute-done.7.refs_10_
  27.4 1.6 collective-permute-start.10
  34.1 11.1 %self_project.1 = (bf16[8,304,768]{2,1,0:T(8,128)(2,1)}, f32[16,768]{1,0:T(8,128)S(1)}, bf16[1024,768]{1,0:T(8,128)(2,1)S(1)}, bf16[1024,768]{1,0:T(8,128)(2,1)}, bf16[1024,768]{1,0:T(8,128)(2,1)}) custom-call(s32[1]{0:T(128)} %bitcast.refs_0_.me_ref, bf16[1024,768]{1,0:T(8,128)(2,1)} %bitcast.19, bf16[304,768]{1,0:T(8,128)(2,1)S(1)} %pack_self.1.refs_2_, ...), custom_call_target="tpu_custom_call" | custom-call | flops 3623878656 | bytes 7864320 | tf_op jit(solution)/shard_map/self_project/pallas_call | solution.py:371
  45.2 1.9 collective-permute-done.12.refs_16_
  47.1 1.9 collective-permute-done.11.refs_15_
  52.1 7.4 %collective-permute-done.14.refs_19_ = bf16[208,768]{1,0:T(8,128)(2,1)S(1)} collective-permute-done((bf16[208,768]{1,0:T(8,128)(2,1)S(1)}, bf16[208,768]{1,0:T(8,128)(2,1)S(1)}, u32[]{:S(2)}, u32[]{:S(2)}) %collective-permute-start.14) | collective-permute-done | bytes 319520 | tf_op jit(solution)/shard_map/ppermute | solution.py:666
  60.7 1.4 copy-done.43
  62.2 1.4 copy-done.45
  63.6 12.3 %attend_forward.2 = (bf16[1024,768]{1,0:T(8,128)(2,1)S(1)}, f32[6,2,1024]{2,1,0:T(2,128)S(1)}) custom-call(s32[1]{0:T(128)S(6)} %copy.32.refs_0_, bf16[1024,768]{1,0:T(8,128)(2,1)S(1)} %get-tuple-element.174.refs_1_, bf16[1024,768]{1,0:T(8,128)(2,1)S(1)} %copy-done.43, bf16[1024,768]{1,0:T(8,128)(2,1)S(1)} %copy-done.45), custom_call_target="tpu_custom_call" | custom-call | flops 8053063680 | bytes 6291456 | tf_op jit(solution)/shard_map/attend_forward/pallas_call | solution.py:187
  82.4 11.6 %self_out_cross_project.1 = (bf16[8,288,768]{2,1,0:T(8,128)(2,1)}, bf16[8,208,768]{2,1,0:T(8,128)(2,1)}, f32[1024,768]{1,0:T(8,128)}, f32[1024,1]{1,0:T(8,128)},...) custom-call(s32[1]{0:T(128)} %bitcast.refs_0_.me_ref, ...), custom_call_target="tpu_custom_call" | custom-call | flops 4831838208 | bytes 14155776 | tf_op jit(solution)/shard_map/self_out_cross_project/pallas_call | solution.py:412
  94.6 11.3 %collective-permute-done.26.refs_17_ = bf16[384,768]{1,0:T(8,128)(2,1)S(1)} collective-permute-done((bf16[384,768]{1,0:T(8,128)(2,1)S(1)}, bf16[384,768]{1,0:T(8,128)(2,1)S(1)}, u32[]{:S(2)}, u32[]{:S(2)}) %collective-permute-start.26) | collective-permute-done | bytes 589856 | tf_op jit(solution)/shard_map/ppermute | solution.py:666
  108.2 1.4 copy-done.33
  109.6 1.4 copy-done.35
  111.0 1.4 copy-done.37
  112.4 19.9 %attend_forward.3 = (bf16[1024,768]{1,0:T(8,128)(2,1)S(1)}, f32[6,2,1024]{2,1,0:T(2,128)S(1)}) custom-call(s32[1]{0:T(128)S(6)} %copy.33.refs_0_, bf16[1024,768]{1,0:T(8,128)(2,1)S(1)} %copy-done.33, bf16[1024,768]{1,0:T(8,128)(2,1)S(1)} %copy-done.35, bf16[1024,768]{1,0:T(8,128)(2,1)S(1)} %copy-done.37), custom_call_target="tpu_custom_call" | custom-call | flops 12884901888 | bytes 6291456 | tf_op jit(solution)/shard_map/attend_forward/pallas_call | solution.py:187
  134.8 2.4 collective-permute-done.35.refs_19_
  139.8 46.0 %ffn.1 = (bf16[1024,768]{1,0:T(8,128)(2,1)}, bf16[1024,3072]{1,0:T(8,128)(2,1)}, bf16[1024,3072]{1,0:T(8,128)(2,1)}, bf16[1024,768]{1,0:T(8,128)(2,1)}, bf16[102...) custom-call(s32[1]{0:T(128)} %bitcast.refs_0_.me_ref, ...), custom_call_target="tpu_custom_call" | custom-call | flops 21743271936 | bytes 15728640 | tf_op jit(solution)/shard_map/ffn/pallas_call | solution.py:510
  185.8 10.6 %ffn_out_grad.1 = (bf16[4,384,768]{2,1,0:T(8,128)(2,1)}, bf16[4,384,768]{2,1,0:T(8,128)(2,1)}) custom-call(s32[1]{0:T(128)} %bitcast.refs_0_.me_ref, bf16[1024,3072]{1,0:T(8,128)(2,1)} %get-tuple-element.204.left, bf16[1024,768]{1,0:T(8,128)(2,1)} %get-tuple-element.205.right), custom_call_target="tpu_custom_call" | custom-call | flops 4831838208 | bytes 14155776 | tf_op jit(solution)/shard_map/ffn_out_grad/pallas_call | solution.py:653
  196.5 11.1 %ffn_in_grad.1 = (bf16[4,384,768]{2,1,0:T(8,128)(2,1)}, bf16[4,384,768]{2,1,0:T(8,128)(2,1)}) custom-call(s32[1]{0:T(128)} %bitcast.refs_0_.me_ref, bf16[1024,768]{1,0:T(8,128)(2,1)} %get-tuple-element.210.refs_1_, bf16[1024,3072]{1,0:T(8,128)(2,1)} %get-tuple-element.211.refs_2_), custom_call_target="tpu_custom_call" | custom-call | flops 4831838208 | bytes 7864320 | tf_op jit(solution)/shard_map/ffn_in_grad/pallas_call | solution.py:626
  208.0 1.4 copy-done.50
  209.4 2.3 grad_split.4
  211.8 1.5 collective-permute-start.38
  215.3 1.4 copy-done.38
  216.7 1.4 copy-done.40
  219.6 35.1 %attend_backward.2 = (bf16[1024,768]{1,0:T(8,128)(2,1)S(1)}, bf16[1024,768]{1,0:T(8,128)(2,1)S(1)}, bf16[1024,768]{1,0:T(8,128)(2,1)S(1)}, f32[8,768]{1,0:T(8,128)S(1)}) custom-call(s32[1]{0:T(128)S(6)} %copy.33.refs_0_, bf16[1024,768]{1,0:T(8,128)(2,1)S(1)} %copy-done.34, bf16[1024,768]{1,0:T(8,128)(2,1)S(1)} %copy-done.36, ...), custom_call_target="tpu_custom_call" | custom-call | flops 32212254720 | bytes 12582912 | tf_op jit(solution)/shard_map/attend_backward/pallas_call | solution.py:209
  257.4 3.7 collective-permute-start.45
  261.9 2.2 grad_split.5
  264.1 10.0 %cross_query_back.1 = (f32[1024,768]{1,0:T(8,128)}, bf16[1024,768]{1,0:T(8,128)(2,1)S(1)}, bf16[1024,768]{1,0:T(8,128)(2,1)S(1)}, f32[8,768]{1,0:T(8,128)S(1)}) custom-call(f32[16,768]{1,0:T(8,128)S(1)} %copy-done.19, bf16[1024,768]{1,0:T(8,128)(2,1)S(1)} %get-tuple-element.234.dq.refs_2_, f32[1024,768]{1,0:T(8,128)} %get-tuple-element.235.dy, ...), custom_call_target="tpu_custom_call" | custom-call | flops 2415919104 | bytes 20250624 | tf_op jit(solution)/shard_map/cross_query_back/pallas_call | solution.py:546
  275.9 14.6 %cross_grad.1 = (bf16[4,512,768]{2,1,0:T(8,128)(2,1)}, bf16[4,512,768]{2,1,0:T(8,128)(2,1)}) custom-call(s32[1]{0:T(128)} %bitcast.refs_0_.me_ref, bf16[1024,768]{1,0:T(8,128)(2,1)} %get-tuple-element.243.refs_1_, bf16[1024,768]{1,0:T(8,128)(2,1)} %copy-done.13, bf16[1024,768]{1,0:T(8,128)(2,1)} %bitcast.18, bf16[1024,768]{1,0:T(8,128)(2,1)} %copy-done.3, ...), custom_call_target="tpu_custom_call" | custom-call | flops 6039797760 | bytes 14155776 | tf_op jit(solution)/shard_map/cross_grad/pallas_call | solution.py:626
  290.5 1.4 collective-permute-start.42
  294.1 13.5 %collective-permute-done.42.far = bf16[384,768]{1,0:T(8,128)(2,1)S(1)} collective-permute-done((bf16[384,768]{1,0:T(8,128)(2,1)S(1)}, bf16[384,768]{1,0:T(8,128)(2,1)S(1)}, u32[]{:S(2)}, u32[]{:S(2)}) %collective-permute-start.42) | collective-permute-done | bytes 589856 | tf_op jit(solution)/shard_map/ppermute | solution.py:666
  307.6 11.9 %collective-permute-done.43.from_x = bf16[384,768]{1,0:T(8,128)(2,1)S(1)} collective-permute-done((bf16[384,768]{1,0:T(8,128)(2,1)S(1)}, bf16[384,768]{1,0:T(8,128)(2,1)S(1)}, u32[]{:S(2)}, u32[]{:S(2)}) %collective-permute-start.43) | collective-permute-done | bytes 589856 | tf_op jit(solution)/shard_map/ppermute | solution.py:666
  320.0 3.7 collective-permute-start.48
  325.9 23.6 %attend_backward.3 = (bf16[1024,768]{1,0:T(8,128)(2,1)S(1)}, bf16[1024,768]{1,0:T(8,128)(2,1)S(1)}, bf16[1024,768]{1,0:T(8,128)(2,1)S(1)}, f32[8,768]{1,0:T(8,128)S(1)}) custom-call(s32[1]{0:T(128)S(6)} %copy.32.refs_0_, bf16[1024,768]{1,0:T(8,128)(2,1)S(1)} %copy-done.42, bf16[1024,768]{1,0:T(8,128)(2,1)S(1)} %copy-done.44, ...), custom_call_target="tpu_custom_call" | custom-call | flops 20132659200 | bytes 12582912 | tf_op jit(solution)/shard_map/attend_backward/pallas_call | solution.py:209
  353.6 8.8 %self_grad.1 = (bf16[4,320,768]{2,1,0:T(8,128)(2,1)}, bf16[4,320,768]{2,1,0:T(8,128)(2,1)}) custom-call(s32[1]{0:T(128)} %bitcast.refs_0_.me_ref, bf16[1024,768]{1,0:T(8,128)(2,1)} %bitcast.21, bf16[1024,768]{1,0:T(8,128)(2,1)} %copy-done.7, bf16[1024,768]{1,0:T(8,128)(2,1)} %copy-done.9, bf16[1024,768]{1,0:T(8,128)(2,1)} %copy-done.11, f32[8,768]{1,0:T(8,128)} %copy-done.47), custom_call_target="tpu_custom_call" | custom-call | flops 3623878656 | bytes 6291456 | tf_op jit(solution)/shard_map/self_grad/pallas_call | solution.py:626
  362.5 3.6 grad_split.6
  366.1 1.6 collective-permute-start.62
  370.9 16.6 %collective-permute-done.62.far = bf16[512,768]{1,0:T(8,128)(2,1)S(1)} collective-permute-done((bf16[512,768]{1,0:T(8,128)(2,1)S(1)}, bf16[512,768]{1,0:T(8,128)(2,1)S(1)}, u32[]{:S(2)}, u32[]{:S(2)}) %collective-permute-start.62) | collective-permute-done | bytes 786464 | tf_op jit(solution)/shard_map/ppermute | solution.py:666
  387.4 2.2 collective-permute-start.75
  389.6 14.0 %collective-permute-done.63.from_x = bf16[512,768]{1,0:T(8,128)(2,1)S(1)} collective-permute-done((bf16[512,768]{1,0:T(8,128)(2,1)S(1)}, bf16[512,768]{1,0:T(8,128)(2,1)S(1)}, u32[]{:S(2)}, u32[]{:S(2)}) %collective-permute-start.63) | collective-permute-done | bytes 786464 | tf_op jit(solution)/shard_map/ppermute | solution.py:666
  404.2 3.7 collective-permute-start.65
  407.9 8.2 %self_project_back.1 = f32[1024,768]{1,0:T(8,128)} custom-call(bf16[1024,768]{1,0:T(8,128)(2,1)S(1)} %copy-done.8, bf16[1024,768]{1,0:T(8,128)(2,1)S(1)} %copy-done.10, bf16[1024,768]{1,0:T(8,128)(2,1)S(1)} %copy-done.12, f32[1024,768]{1,0:T(8,128)} %get-tuple-element.284.dy, bf16[8,304,768]{2,1,0:T(8,128)(2,1)} %get-tuple-element.285.w), custom_call_target="tpu_custom_call" | custom-call | flops 3623878656 | bytes 14745600 | tf_op jit(solution)/shard_map/self_project_back/pallas_call | solution.py:585
  417.4 2.0 grad_split.7
  419.3 1.6 collective-permute-start.53
  423.7 8.7 %collective-permute-done.66.two = bf16[128,768]{1,0:T(8,128)(2,1)S(1)} collective-permute-done((bf16[128,768]{1,0:T(8,128)(2,1)S(1)}, bf16[128,768]{1,0:T(8,128)(2,1)S(1)}, u32[]{:S(2)}, u32[]{:S(2)}) %collective-permute-start.66) | collective-permute-done | bytes 196640 | tf_op jit(solution)/shard_map/ppermute | solution.py:666
  432.4 1.8 collective-permute-start.74
  434.4 6.6 %collective-permute-done.74.refs_2_ = bf16[96,768]{1,0:T(8,128)(2,1)S(1)} collective-permute-done((bf16[96,768]{1,0:T(8,128)(2,1)S(1)}, bf16[96,768]{1,0:T(8,128)(2,1)S(1)}, u32[]{:S(2)}, u32[]{:S(2)}) %collective-permute-start.74) | collective-permute-done | bytes 147488 | tf_op jit(solution)/shard_map/ppermute | solution.py:666
  440.9 1.8 collective-permute-done.73.refs_4_
  442.7 1.9 collective-permute-start.72
  446.6 2.0 collective-permute-start.68
  448.8 15.4 %collective-permute-done.72.refs_3_ = bf16[96,768]{1,0:T(8,128)(2,1)S(1)} collective-permute-done((bf16[96,768]{1,0:T(8,128)(2,1)S(1)}, bf16[96,768]{1,0:T(8,128)(2,1)S(1)}, u32[]{:S(2)}, u32[]{:S(2)}) %collective-permute-start.72) | collective-permute-done | bytes 147488 | tf_op jit(solution)/shard_map/ppermute | solution.py:666
  465.5 3.9 collective-permute-start.57
  469.4 1.5 collective-permute-start.58
  473.3 3.6 collective-permute-done.69.refs_3_
  478.1 6.6 %collective-permute-done.57.two = bf16[80,768]{1,0:T(8,128)(2,1)S(1)} collective-permute-done((bf16[80,768]{1,0:T(8,128)(2,1)S(1)}, bf16[80,768]{1,0:T(8,128)(2,1)S(1)}, u32[]{:S(2)}, u32[]{:S(2)}) %collective-permute-start.57) | collective-permute-done | bytes 122912 | tf_op jit(solution)/shard_map/ppermute | solution.py:666
  484.8 2.4 collective-permute-start.60
  487.2 2.0 collective-permute-start.59
  489.2 6.2 %memory_back.1 = f32[1024,768]{1,0:T(8,128)} custom-call(bf16[1024,768]{1,0:T(8,128)(2,1)S(1)} %copy-done.4, bf16[1024,768]{1,0:T(8,128)(2,1)S(1)} %copy-done.6, bf16[8,288,768]{2,1,0:T(8,128)(2,1)} %get-tuple-element.237.w), custom_call_target="tpu_custom_call" | custom-call | flops 2415919104 | bytes 9830400 | tf_op jit(solution)/shard_map/memory_back/pallas_call | solution.py:565
  (263 shorter events, 63.8 us)
Async XLA Ops:
  5.2 13.7 %collective-permute-start.2 = (bf16[304,768]{1,0:T(8,128)(2,1)S(1)}, bf16[304,768]{1,0:T(8,128)(2,1)S(1)}, u32[]{:S(2)}, u32[]{:S(2)}) collective-permute-start(bf16[304,768]{1,0:T(8,128)(2,1)S(1)} %pack_self.1.refs_2_), channel_id=1, source_target_pairs={{0,16},{4,20},{8,24},{12,28},{16,0},{20,4},{24,8},{28,12},{1,17},{... | collective-permute-start | bytes 1400840 | tf_op jit(solution)/shard_map/ppermute | solution.py:666
  8.2 12.5 %collective-permute-start.1 = (bf16[304,768]{1,0:T(8,128)(2,1)S(1)}, bf16[304,768]{1,0:T(8,128)(2,1)S(1)}, u32[]{:S(2)}, u32[]{:S(2)}) collective-permute-start(bf16[304,768]{1,0:T(8,128)(2,1)S(1)} %pack_self.1.refs_2_), channel_id=1, source_target_pairs={{0,8},{4,12},{8,0},{12,4},{16,24},{20,28},{24,16},{28,20},{1,9},{5... | collective-permute-start | bytes 1400840 | tf_op jit(solution)/shard_map/ppermute | solution.py:666
  9.7 17.7 %collective-permute-start = (bf16[304,768]{1,0:T(8,128)(2,1)S(1)}, bf16[304,768]{1,0:T(8,128)(2,1)S(1)}, u32[]{:S(2)}, u32[]{:S(2)}) collective-permute-start(bf16[304,768]{1,0:T(8,128)(2,1)S(1)} %pack_self.1.refs_2_), channel_id=1, source_target_pairs={{0,4},{4,0},{8,12},{12,8},{16,20},{20,16},{24,28},{28,24},{1,5},{5... | collective-permute-start | bytes 1400840 | tf_op jit(solution)/shard_map/ppermute | solution.py:666
  22.3 9.0 %collective-permute-start.3 = (bf16[304,768]{1,0:T(8,128)(2,1)S(1)}, bf16[304,768]{1,0:T(8,128)(2,1)S(1)}, u32[]{:S(2)}, u32[]{:S(2)}) collective-permute-start(bf16[304,768]{1,0:T(8,128)(2,1)S(1)} %collective-permute-done.1.refs_4_), channel_id=1, source_target_pairs={{0,4},{4,0},{8,12},{12,8},{16,20},{20,16},{24,28},{28,24},{1,5},{5... | collective-permute-start | bytes 1400840 | tf_op jit(solution)/shard_map/ppermute | solution.py:666
  27.4 21.6 %collective-permute-start.10 = (bf16[288,768]{1,0:T(8,128)(2,1)}, bf16[288,768]{1,0:T(8,128)(2,1)}, u32[]{:S(2)}, u32[]{:S(2)}) collective-permute-start(bf16[288,768]{1,0:T(8,128)(2,1)} %bitcast.3.refs_5_), channel_id=1, source_target_pairs={{0,16},{4,20},{8,24},{12,28},{16,0},{20,4},{24,8},{28,12},{1,17},{... | collective-permute-start | bytes 1327112 | tf_op jit(solution)/shard_map/ppermute | solution.py:666
  29.7 19.4 %collective-permute-start.9 = (bf16[288,768]{1,0:T(8,128)(2,1)}, bf16[288,768]{1,0:T(8,128)(2,1)}, u32[]{:S(2)}, u32[]{:S(2)}) collective-permute-start(bf16[288,768]{1,0:T(8,128)(2,1)} %bitcast.3.refs_5_), channel_id=1, source_target_pairs={{0,8},{4,12},{8,0},{12,4},{16,24},{20,28},{24,16},{28,20},{1,9},{5... | collective-permute-start | bytes 1327112 | tf_op jit(solution)/shard_map/ppermute | solution.py:666
  30.2 16.9 %collective-permute-start.12 = (bf16[208,768]{1,0:T(8,128)(2,1)S(1)}, bf16[208,768]{1,0:T(8,128)(2,1)S(1)}, u32[]{:S(2)}, u32[]{:S(2)}) collective-permute-start(bf16[208,768]{1,0:T(8,128)(2,1)S(1)} %pack_out.1.refs_13_), channel_id=1, source_target_pairs={{0,16},{4,20},{8,24},{12,28},{16,0},{20,4},{24,8},{28,12},{1,17},{... | collective-permute-start | bytes 958472 | tf_op jit(solution)/shard_map/ppermute | solution.py:666
  31.3 17.7 %collective-permute-start.11 = (bf16[208,768]{1,0:T(8,128)(2,1)S(1)}, bf16[208,768]{1,0:T(8,128)(2,1)S(1)}, u32[]{:S(2)}, u32[]{:S(2)}) collective-permute-start(bf16[208,768]{1,0:T(8,128)(2,1)S(1)} %pack_out.1.refs_13_), channel_id=1, source_target_pairs={{0,8},{4,12},{8,0},{12,4},{16,24},{20,28},{24,16},{28,20},{1,9},{5... | collective-permute-start | bytes 958472 | tf_op jit(solution)/shard_map/ppermute | solution.py:666
  49.1 11.7 %collective-permute-start.13 = (bf16[288,768]{1,0:T(8,128)(2,1)}, bf16[288,768]{1,0:T(8,128)(2,1)S(1)}, u32[]{:S(2)}, u32[]{:S(2)}) collective-permute-start(bf16[288,768]{1,0:T(8,128)(2,1)} %collective-permute-done.10.refs_8_), channel_id=1, source_target_pairs={{0,8},{4,12},{8,0},{12,4},{16,24},{20,28},{24,16},{28,20},{1,9},{5... | collective-permute-start | bytes 1327112 | tf_op jit(solution)/shard_map/ppermute | solution.py:666
  49.6 9.9 %collective-permute-start.14 = (bf16[208,768]{1,0:T(8,128)(2,1)S(1)}, bf16[208,768]{1,0:T(8,128)(2,1)S(1)}, u32[]{:S(2)}, u32[]{:S(2)}) collective-permute-start(bf16[208,768]{1,0:T(8,128)(2,1)S(1)} %collective-permute-done.11.refs_15_), channel_id=1, source_target_pairs={{0,16},{4,20},{8,24},{12,28},{16,0},{20,4},{24,8},{28,12},{1,17},{... | collective-permute-start | bytes 958472 | tf_op jit(solution)/shard_map/ppermute | solution.py:666
  51.3 25.7 %collective-permute-start.15 = (bf16[288,768]{1,0:T(8,128)(2,1)}, bf16[288,768]{1,0:T(8,128)(2,1)S(1)}, u32[]{:S(2)}, u32[]{:S(2)}) collective-permute-start(bf16[288,768]{1,0:T(8,128)(2,1)} %bitcast.3.refs_5_), channel_id=1, source_target_pairs={{0,4},{4,0},{8,12},{12,8},{16,20},{20,16},{24,28},{28,24},{1,5},{5... | collective-permute-start | bytes 1327112 | tf_op jit(solution)/shard_map/ppermute | solution.py:666
  51.6 25.9 %collective-permute-start.20 = (bf16[208,768]{1,0:T(8,128)(2,1)S(1)}, bf16[208,768]{1,0:T(8,128)(2,1)S(1)}, u32[]{:S(2)}, u32[]{:S(2)}) collective-permute-start(bf16[208,768]{1,0:T(8,128)(2,1)S(1)} %collective-permute-done.11.refs_15_), channel_id=1, source_target_pairs={{0,4},{4,0},{8,12},{12,8},{16,20},{20,16},{24,28},{28,24},{1,5},{5... | collective-permute-start | bytes 958472 | tf_op jit(solution)/shard_map/ppermute | solution.py:666
  51.9 27.3 %collective-permute-start.17 = (bf16[288,768]{1,0:T(8,128)(2,1)}, bf16[288,768]{1,0:T(8,128)(2,1)S(1)}, u32[]{:S(2)}, u32[]{:S(2)}) collective-permute-start(bf16[288,768]{1,0:T(8,128)(2,1)} %collective-permute-done.10.refs_8_), channel_id=1, source_target_pairs={{0,4},{4,0},{8,12},{12,8},{16,20},{20,16},{24,28},{28,24},{1,5},{5... | collective-permute-start | bytes 1327112 | tf_op jit(solution)/shard_map/ppermute | solution.py:666
  59.5 17.9 %collective-permute-start.21 = (bf16[208,768]{1,0:T(8,128)(2,1)S(1)}, bf16[208,768]{1,0:T(8,128)(2,1)S(1)}, u32[]{:S(2)}, u32[]{:S(2)}) collective-permute-start(bf16[208,768]{1,0:T(8,128)(2,1)S(1)} %collective-permute-done.12.refs_16_), channel_id=1, source_target_pairs={{0,4},{4,0},{8,12},{12,8},{16,20},{20,16},{24,28},{28,24},{1,5},{5... | collective-permute-start | bytes 958472 | tf_op jit(solution)/shard_map/ppermute | solution.py:666
  60.7 17.3 %collective-permute-start.16 = (bf16[288,768]{1,0:T(8,128)(2,1)}, bf16[288,768]{1,0:T(8,128)(2,1)S(1)}, u32[]{:S(2)}, u32[]{:S(2)}) collective-permute-start(bf16[288,768]{1,0:T(8,128)(2,1)} %collective-permute-done.9.refs_7_), channel_id=1, source_target_pairs={{0,4},{4,0},{8,12},{12,8},{16,20},{20,16},{24,28},{28,24},{1,5},{5... | collective-permute-start | bytes 1327112 | tf_op jit(solution)/shard_map/ppermute | solution.py:666
  77.6 16.4 %collective-permute-start.24 = (bf16[96,3072]{1,0:T(8,128)(2,1)S(1)}, bf16[96,3072]{1,0:T(8,128)(2,1)S(1)}, u32[]{:S(2)}, u32[]{:S(2)}) collective-permute-start(bf16[96,3072]{1,0:T(8,128)(2,1)S(1)} %copy-done.52), channel_id=1, source_target_pairs={{0,16},{4,20},{8,24},{12,28},{16,0},{20,4},{24,8},{28,12},{1,17},{... | collective-permute-start | bytes 1769480 | tf_op jit(solution)/shard_map/ppermute | solution.py:666
  78.1 16.5 %collective-permute-start.23 = (bf16[96,3072]{1,0:T(8,128)(2,1)S(1)}, bf16[96,3072]{1,0:T(8,128)(2,1)S(1)}, u32[]{:S(2)}, u32[]{:S(2)}) collective-permute-start(bf16[96,3072]{1,0:T(8,128)(2,1)S(1)} %copy-done.52), channel_id=1, source_target_pairs={{0,8},{4,12},{8,0},{12,4},{16,24},{20,28},{24,16},{28,20},{1,9},{5... | collective-permute-start | bytes 1769480 | tf_op jit(solution)/shard_map/ppermute | solution.py:666
  79.2 26.7 %collective-permute-start.26 = (bf16[384,768]{1,0:T(8,128)(2,1)S(1)}, bf16[384,768]{1,0:T(8,128)(2,1)S(1)}, u32[]{:S(2)}, u32[]{:S(2)}) collective-permute-start(bf16[384,768]{1,0:T(8,128)(2,1)S(1)} %copy-done.53), channel_id=1, source_target_pairs={{0,16},{4,20},{8,24},{12,28},{16,0},{20,4},{24,8},{28,12},{1,17},{... | collective-permute-start | bytes 1769480 | tf_op jit(solution)/shard_map/ppermute | solution.py:666
  80.4 25.8 %collective-permute-start.25 = (bf16[384,768]{1,0:T(8,128)(2,1)S(1)}, bf16[384,768]{1,0:T(8,128)(2,1)S(1)}, u32[]{:S(2)}, u32[]{:S(2)}) collective-permute-start(bf16[384,768]{1,0:T(8,128)(2,1)S(1)} %copy-done.53), channel_id=1, source_target_pairs={{0,8},{4,12},{8,0},{12,4},{16,24},{20,28},{24,16},{28,20},{1,9},{5... | collective-permute-start | bytes 1769480 | tf_op jit(solution)/shard_map/ppermute | solution.py:666
  82.3 51.8 %collective-permute-start.29 = (bf16[96,3072]{1,0:T(8,128)(2,1)S(1)}, bf16[96,3072]{1,0:T(8,128)(2,1)S(1)}, u32[]{:S(2)}, u32[]{:S(2)}) collective-permute-start(bf16[96,3072]{1,0:T(8,128)(2,1)S(1)} %copy-done.52), channel_id=1, source_target_pairs={{0,4},{4,0},{8,12},{12,8},{16,20},{20,16},{24,28},{28,24},{1,5},{5... | collective-permute-start | bytes 1769480 | tf_op jit(solution)/shard_map/ppermute | solution.py:666
  94.0 40.2 %collective-permute-start.33 = (bf16[384,768]{1,0:T(8,128)(2,1)S(1)}, bf16[384,768]{1,0:T(8,128)(2,1)S(1)}, u32[]{:S(2)}, u32[]{:S(2)}) collective-permute-start(bf16[384,768]{1,0:T(8,128)(2,1)S(1)} %copy-done.53), channel_id=1, source_target_pairs={{0,4},{4,0},{8,12},{12,8},{16,20},{20,16},{24,28},{28,24},{1,5},{5... | collective-permute-start | bytes 1769480 | tf_op jit(solution)/shard_map/ppermute | solution.py:666
  106.1 28.6 %collective-permute-start.30 = (bf16[96,3072]{1,0:T(8,128)(2,1)S(1)}, bf16[96,3072]{1,0:T(8,128)(2,1)S(1)}, u32[]{:S(2)}, u32[]{:S(2)}) collective-permute-start(bf16[96,3072]{1,0:T(8,128)(2,1)S(1)} %collective-permute-done.23.refs_8_), channel_id=1, source_target_pairs={{0,4},{4,0},{8,12},{12,8},{16,20},{20,16},{24,28},{28,24},{1,5},{5... | collective-permute-start | bytes 1769480 | tf_op jit(solution)/shard_map/ppermute | solution.py:666
  106.1 27.4 %collective-permute-start.27 = (bf16[96,3072]{1,0:T(8,128)(2,1)S(1)}, bf16[96,3072]{1,0:T(8,128)(2,1)S(1)}, u32[]{:S(2)}, u32[]{:S(2)}) collective-permute-start(bf16[96,3072]{1,0:T(8,128)(2,1)S(1)} %collective-permute-done.24.refs_9_), channel_id=1, source_target_pairs={{0,8},{4,12},{8,0},{12,4},{16,24},{20,28},{24,16},{28,20},{1,9},{5... | collective-permute-start | bytes 1769480 | tf_op jit(solution)/shard_map/ppermute | solution.py:666
  107.3 26.3 %collective-permute-start.28 = (bf16[384,768]{1,0:T(8,128)(2,1)S(1)}, bf16[384,768]{1,0:T(8,128)(2,1)S(1)}, u32[]{:S(2)}, u32[]{:S(2)}) collective-permute-start(bf16[384,768]{1,0:T(8,128)(2,1)S(1)} %collective-permute-done.25.refs_16_), channel_id=1, source_target_pairs={{0,16},{4,20},{8,24},{12,28},{16,0},{20,4},{24,8},{28,12},{1,17},{... | collective-permute-start | bytes 1769480 | tf_op jit(solution)/shard_map/ppermute | solution.py:666
  196.4 11.6 %collective-permute-start.37 = (bf16[4,384,768]{2,1,0:T(8,128)(2,1)}, bf16[4,384,768]{2,1,0:T(8,128)(2,1)S(1)}, u32[]{:S(2)}, u32[]{:S(2)}) collective-permute-start(bf16[4,384,768]{2,1,0:T(8,128)(2,1)} %get-tuple-element.208), channel_id=1, source_target_pairs={{0,4},{4,0},{8,12},{12,8},{16,20},{20,16},{24,28},{28,24},{1,5},{5... | collective-permute-start | bytes 7077896 | tf_op jit(solution)/shard_map/ppermute | solution.py:666
  207.6 49.5 %collective-permute-start.41 = (bf16[4,384,768]{2,1,0:T(8,128)(2,1)}, bf16[4,384,768]{2,1,0:T(8,128)(2,1)}, u32[]{:S(2)}, u32[]{:S(2)}) collective-permute-start(bf16[4,384,768]{2,1,0:T(8,128)(2,1)} %get-tuple-element.224), channel_id=1, source_target_pairs={{0,4},{4,0},{8,12},{12,8},{16,20},{20,16},{24,28},{28,24},{1,5},{5... | collective-permute-start | bytes 7077896 | tf_op jit(solution)/shard_map/ppermute | solution.py:666
  211.8 45.3 %collective-permute-start.38 = (bf16[384,768]{1,0:T(8,128)(2,1)S(1)}, bf16[384,768]{1,0:T(8,128)(2,1)S(1)}, u32[]{:S(2)}, u32[]{:S(2)}) collective-permute-start(bf16[384,768]{1,0:T(8,128)(2,1)S(1)} %get-tuple-element.220), channel_id=1, source_target_pairs={{0,24},{4,28},{8,16},{12,20},{16,8},{20,12},{24,0},{28,4},{1,25},{... | collective-permute-start | bytes 1769480 | tf_op jit(solution)/shard_map/ppermute | solution.py:666
  213.3 43.8 %collective-permute-start.39 = (bf16[384,768]{1,0:T(8,128)(2,1)S(1)}, bf16[384,768]{1,0:T(8,128)(2,1)S(1)}, u32[]{:S(2)}, u32[]{:S(2)}) collective-permute-start(bf16[384,768]{1,0:T(8,128)(2,1)S(1)} %get-tuple-element.221), channel_id=1, source_target_pairs={{0,8},{4,12},{8,0},{12,4},{16,24},{20,28},{24,16},{28,20},{1,9},{5... | collective-permute-start | bytes 1769480 | tf_op jit(solution)/shard_map/ppermute | solution.py:666
  214.4 42.7 %collective-permute-start.40 = (bf16[384,768]{1,0:T(8,128)(2,1)S(1)}, bf16[384,768]{1,0:T(8,128)(2,1)S(1)}, u32[]{:S(2)}, u32[]{:S(2)}) collective-permute-start(bf16[384,768]{1,0:T(8,128)(2,1)S(1)} %get-tuple-element.222), channel_id=1, source_target_pairs={{0,16},{4,20},{8,24},{12,28},{16,0},{20,4},{24,8},{28,12},{1,17},{... | collective-permute-start | bytes 1769480 | tf_op jit(solution)/shard_map/ppermute | solution.py:666
  257.4 18.4 %collective-permute-start.45 = (bf16[96,768]{1,0:T(8,128)(2,1)S(1)}, bf16[96,768]{1,0:T(8,128)(2,1)S(1)}, u32[]{:S(2)}, u32[]{:S(2)}) collective-permute-start(bf16[96,768]{1,0:T(8,128)(2,1)S(1)} %get-tuple-element.249), channel_id=1, source_target_pairs={{0,3},{1,2},{2,1},{3,0},{4,7},{5,6},{6,5},{7,4},{8,11},{9,10},{10,... | collective-permute-start | bytes 442376 | tf_op jit(solution)/shard_map/ppermute | solution.py:666
  261.1 14.8 %collective-permute-start.46 = (bf16[96,768]{1,0:T(8,128)(2,1)S(1)}, bf16[96,768]{1,0:T(8,128)(2,1)S(1)}, u32[]{:S(2)}, u32[]{:S(2)}) collective-permute-start(bf16[96,768]{1,0:T(8,128)(2,1)S(1)} %get-tuple-element.250), channel_id=1, source_target_pairs={{0,2},{1,3},{2,0},{3,1},{4,6},{5,7},{6,4},{7,5},{8,10},{9,11},{10,... | collective-permute-start | bytes 442376 | tf_op jit(solution)/shard_map/ppermute | solution.py:666
  261.1 14.8 %collective-permute-start.47 = (bf16[96,768]{1,0:T(8,128)(2,1)S(1)}, bf16[96,768]{1,0:T(8,128)(2,1)S(1)}, u32[]{:S(2)}, u32[]{:S(2)}) collective-permute-start(bf16[96,768]{1,0:T(8,128)(2,1)S(1)} %get-tuple-element.251), channel_id=1, source_target_pairs={{0,1},{1,0},{2,3},{3,2},{4,5},{5,4},{6,7},{7,6},{8,9},{9,8},{10,11... | collective-permute-start | bytes 442376 | tf_op jit(solution)/shard_map/ppermute | solution.py:666
  290.5 63.2 %collective-permute-start.51 = (bf16[4,512,768]{2,1,0:T(8,128)(2,1)}, bf16[4,512,768]{2,1,0:T(8,128)(2,1)}, u32[]{:S(2)}, u32[]{:S(2)}) collective-permute-start(bf16[4,512,768]{2,1,0:T(8,128)(2,1)} %get-tuple-element.274), channel_id=1, source_target_pairs={{0,4},{4,0},{8,12},{12,8},{16,20},{20,16},{24,28},{28,24},{1,5},{5... | collective-permute-start | bytes 9437192 | tf_op jit(solution)/shard_map/ppermute | solution.py:666
  290.5 17.1 %collective-permute-start.42 = (bf16[384,768]{1,0:T(8,128)(2,1)S(1)}, bf16[384,768]{1,0:T(8,128)(2,1)S(1)}, u32[]{:S(2)}, u32[]{:S(2)}) collective-permute-start(bf16[384,768]{1,0:T(8,128)(2,1)S(1)} %get-tuple-element.240), channel_id=1, source_target_pairs={{0,24},{4,28},{8,16},{12,20},{16,8},{20,12},{24,0},{28,4},{1,25},{... | collective-permute-start | bytes 1769480 | tf_op jit(solution)/shard_map/ppermute | solution.py:666
  291.9 27.5 %collective-permute-start.43 = (bf16[384,768]{1,0:T(8,128)(2,1)S(1)}, bf16[384,768]{1,0:T(8,128)(2,1)S(1)}, u32[]{:S(2)}, u32[]{:S(2)}) collective-permute-start(bf16[384,768]{1,0:T(8,128)(2,1)S(1)} %get-tuple-element.241), channel_id=1, source_target_pairs={{0,8},{4,12},{8,0},{12,4},{16,24},{20,28},{24,16},{28,20},{1,9},{5... | collective-permute-start | bytes 1769480 | tf_op jit(solution)/shard_map/ppermute | solution.py:666
  293.1 26.7 %collective-permute-start.44 = (bf16[384,768]{1,0:T(8,128)(2,1)S(1)}, bf16[384,768]{1,0:T(8,128)(2,1)S(1)}, u32[]{:S(2)}, u32[]{:S(2)}) collective-permute-start(bf16[384,768]{1,0:T(8,128)(2,1)S(1)} %get-tuple-element.242), channel_id=1, source_target_pairs={{0,16},{4,20},{8,24},{12,28},{16,0},{20,4},{24,8},{28,12},{1,17},{... | collective-permute-start | bytes 1769480 | tf_op jit(solution)/shard_map/ppermute | solution.py:666
  320.0 33.6 %collective-permute-start.48 = (bf16[96,768]{1,0:T(8,128)(2,1)S(1)}, bf16[96,768]{1,0:T(8,128)(2,1)S(1)}, u32[]{:S(2)}, u32[]{:S(2)}) collective-permute-start(bf16[96,768]{1,0:T(8,128)(2,1)S(1)} %get-tuple-element.271), channel_id=1, source_target_pairs={{0,3},{1,2},{2,1},{3,0},{4,7},{5,6},{6,5},{7,4},{8,11},{9,10},{10,... | collective-permute-start | bytes 442376 | tf_op jit(solution)/shard_map/ppermute | solution.py:666
  323.7 29.9 %collective-permute-start.49 = (bf16[96,768]{1,0:T(8,128)(2,1)S(1)}, bf16[96,768]{1,0:T(8,128)(2,1)S(1)}, u32[]{:S(2)}, u32[]{:S(2)}) collective-permute-start(bf16[96,768]{1,0:T(8,128)(2,1)S(1)} %get-tuple-element.272), channel_id=1, source_target_pairs={{0,2},{1,3},{2,0},{3,1},{4,6},{5,7},{6,4},{7,5},{8,10},{9,11},{10,... | collective-permute-start | bytes 442376 | tf_op jit(solution)/shard_map/ppermute | solution.py:666
  323.7 29.9 %collective-permute-start.50 = (bf16[96,768]{1,0:T(8,128)(2,1)S(1)}, bf16[96,768]{1,0:T(8,128)(2,1)S(1)}, u32[]{:S(2)}, u32[]{:S(2)}) collective-permute-start(bf16[96,768]{1,0:T(8,128)(2,1)S(1)} %get-tuple-element.273), channel_id=1, source_target_pairs={{0,1},{1,0},{2,3},{3,2},{4,5},{5,4},{6,7},{7,6},{8,9},{9,8},{10,11... | collective-permute-start | bytes 442376 | tf_op jit(solution)/shard_map/ppermute | solution.py:666
  362.5 53.6 %collective-permute-start.52 = (bf16[4,320,768]{2,1,0:T(8,128)(2,1)}, bf16[4,320,768]{2,1,0:T(8,128)(2,1)S(1)}, u32[]{:S(2)}, u32[]{:S(2)}) collective-permute-start(bf16[4,320,768]{2,1,0:T(8,128)(2,1)} %get-tuple-element.288), channel_id=1, source_target_pairs={{0,4},{4,0},{8,12},{12,8},{16,20},{20,16},{24,28},{28,24},{1,5},{5... | collective-permute-start | bytes 5898248 | tf_op jit(solution)/shard_map/ppermute | solution.py:666
  366.1 21.3 %collective-permute-start.62 = (bf16[512,768]{1,0:T(8,128)(2,1)S(1)}, bf16[512,768]{1,0:T(8,128)(2,1)S(1)}, u32[]{:S(2)}, u32[]{:S(2)}) collective-permute-start(bf16[512,768]{1,0:T(8,128)(2,1)S(1)} %get-tuple-element.303), channel_id=1, source_target_pairs={{0,24},{4,28},{8,16},{12,20},{16,8},{20,12},{24,0},{28,4},{1,25},{... | collective-permute-start | bytes 2359304 | tf_op jit(solution)/shard_map/ppermute | solution.py:666
  367.7 35.8 %collective-permute-start.63 = (bf16[512,768]{1,0:T(8,128)(2,1)S(1)}, bf16[512,768]{1,0:T(8,128)(2,1)S(1)}, u32[]{:S(2)}, u32[]{:S(2)}) collective-permute-start(bf16[512,768]{1,0:T(8,128)(2,1)S(1)} %get-tuple-element.304), channel_id=1, source_target_pairs={{0,8},{4,12},{8,0},{12,4},{16,24},{20,28},{24,16},{28,20},{1,9},{5... | collective-permute-start | bytes 2359304 | tf_op jit(solution)/shard_map/ppermute | solution.py:666
  368.7 35.1 %collective-permute-start.64 = (bf16[512,768]{1,0:T(8,128)(2,1)S(1)}, bf16[512,768]{1,0:T(8,128)(2,1)S(1)}, u32[]{:S(2)}, u32[]{:S(2)}) collective-permute-start(bf16[512,768]{1,0:T(8,128)(2,1)S(1)} %get-tuple-element.305), channel_id=1, source_target_pairs={{0,16},{4,20},{8,24},{12,28},{16,0},{20,4},{24,8},{28,12},{1,17},{... | collective-permute-start | bytes 2359304 | tf_op jit(solution)/shard_map/ppermute | solution.py:666
  369.7 52.3 %collective-permute-start.76 = (bf16[96,768]{1,0:T(8,128)(2,1)S(1)}, bf16[96,768]{1,0:T(8,128)(2,1)S(1)}, u32[]{:S(2)}, u32[]{:S(2)}) collective-permute-start(bf16[96,768]{1,0:T(8,128)(2,1)S(1)} %grad_add.4.refs_1_), channel_id=1, source_target_pairs={{0,1},{1,0},{2,3},{3,2},{4,5},{5,4},{6,7},{7,6},{8,9},{9,8},{10,11... | collective-permute-start | bytes 442376 | tf_op jit(solution)/shard_map/ppermute | solution.py:666
  387.4 35.4 %collective-permute-start.75 = (bf16[96,768]{1,0:T(8,128)(2,1)S(1)}, bf16[96,768]{1,0:T(8,128)(2,1)S(1)}, u32[]{:S(2)}, u32[]{:S(2)}) collective-permute-start(bf16[96,768]{1,0:T(8,128)(2,1)S(1)} %grad_add.4.refs_1_), channel_id=1, source_target_pairs={{0,2},{1,3},{2,0},{3,1},{4,6},{5,7},{6,4},{7,5},{8,10},{9,11},{10,... | collective-permute-start | bytes 442376 | tf_op jit(solution)/shard_map/ppermute | solution.py:666
  404.2 18.7 %collective-permute-start.65 = (bf16[128,768]{1,0:T(8,128)(2,1)S(1)}, bf16[128,768]{1,0:T(8,128)(2,1)S(1)}, u32[]{:S(2)}, u32[]{:S(2)}) collective-permute-start(bf16[128,768]{1,0:T(8,128)(2,1)S(1)} %get-tuple-element.307), channel_id=1, source_target_pairs={{0,3},{1,2},{2,1},{3,0},{4,7},{5,6},{6,5},{7,4},{8,11},{9,10},{10,... | collective-permute-start | bytes 589832 | tf_op jit(solution)/shard_map/ppermute | solution.py:666
  419.3 25.3 %collective-permute-start.53 = (bf16[320,768]{1,0:T(8,128)(2,1)S(1)}, bf16[320,768]{1,0:T(8,128)(2,1)S(1)}, u32[]{:S(2)}, u32[]{:S(2)}) collective-permute-start(bf16[320,768]{1,0:T(8,128)(2,1)S(1)} %get-tuple-element.294), channel_id=1, source_target_pairs={{0,24},{4,28},{8,16},{12,20},{16,8},{20,12},{24,0},{28,4},{1,25},{... | collective-permute-start | bytes 1474568 | tf_op jit(solution)/shard_map/ppermute | solution.py:666
  420.9 24.6 %collective-permute-start.54 = (bf16[320,768]{1,0:T(8,128)(2,1)S(1)}, bf16[320,768]{1,0:T(8,128)(2,1)S(1)}, u32[]{:S(2)}, u32[]{:S(2)}) collective-permute-start(bf16[320,768]{1,0:T(8,128)(2,1)S(1)} %get-tuple-element.295), channel_id=1, source_target_pairs={{0,8},{4,12},{8,0},{12,4},{16,24},{20,28},{24,16},{28,20},{1,9},{5... | collective-permute-start | bytes 1474568 | tf_op jit(solution)/shard_map/ppermute | solution.py:666
  422.0 24.6 %collective-permute-start.55 = (bf16[320,768]{1,0:T(8,128)(2,1)S(1)}, bf16[320,768]{1,0:T(8,128)(2,1)S(1)}, u32[]{:S(2)}, u32[]{:S(2)}) collective-permute-start(bf16[320,768]{1,0:T(8,128)(2,1)S(1)} %get-tuple-element.296), channel_id=1, source_target_pairs={{0,16},{4,20},{8,24},{12,28},{16,0},{20,4},{24,8},{28,12},{1,17},{... | collective-permute-start | bytes 1474568 | tf_op jit(solution)/shard_map/ppermute | solution.py:666
  422.9 9.5 %collective-permute-start.66 = (bf16[128,768]{1,0:T(8,128)(2,1)S(1)}, bf16[128,768]{1,0:T(8,128)(2,1)S(1)}, u32[]{:S(2)}, u32[]{:S(2)}) collective-permute-start(bf16[128,768]{1,0:T(8,128)(2,1)S(1)} %get-tuple-element.308), channel_id=1, source_target_pairs={{0,2},{1,3},{2,0},{3,1},{4,6},{5,7},{6,4},{7,5},{8,10},{9,11},{10,... | collective-permute-start | bytes 589832 | tf_op jit(solution)/shard_map/ppermute | solution.py:666
  422.9 11.3 %collective-permute-start.67 = (bf16[128,768]{1,0:T(8,128)(2,1)S(1)}, bf16[128,768]{1,0:T(8,128)(2,1)S(1)}, u32[]{:S(2)}, u32[]{:S(2)}) collective-permute-start(bf16[128,768]{1,0:T(8,128)(2,1)S(1)} %get-tuple-element.309), channel_id=1, source_target_pairs={{0,1},{1,0},{2,3},{3,2},{4,5},{5,4},{6,7},{7,6},{8,9},{9,8},{10,11... | collective-permute-start | bytes 589832 | tf_op jit(solution)/shard_map/ppermute | solution.py:666
  432.4 8.6 %collective-permute-start.74 = (bf16[96,768]{1,0:T(8,128)(2,1)S(1)}, bf16[96,768]{1,0:T(8,128)(2,1)S(1)}, u32[]{:S(2)}, u32[]{:S(2)}) collective-permute-start(bf16[96,768]{1,0:T(8,128)(2,1)S(1)} %grad_add.4.refs_1_), channel_id=1, source_target_pairs={{0,3},{1,2},{2,1},{3,0},{4,7},{5,6},{6,5},{7,4},{8,11},{9,10},{10,... | collective-permute-start | bytes 442376 | tf_op jit(solution)/shard_map/ppermute | solution.py:666
  434.2 8.5 %collective-permute-start.73 = (bf16[96,768]{1,0:T(8,128)(2,1)S(1)}, bf16[96,768]{1,0:T(8,128)(2,1)S(1)}, u32[]{:S(2)}, u32[]{:S(2)}) collective-permute-start(bf16[96,768]{1,0:T(8,128)(2,1)S(1)} %grad_add.7.refs_1_), channel_id=1, source_target_pairs={{0,1},{1,0},{2,3},{3,2},{4,5},{5,4},{6,7},{7,6},{8,9},{9,8},{10,11... | collective-permute-start | bytes 442376 | tf_op jit(solution)/shard_map/ppermute | solution.py:666
  440.9 28.5 %collective-permute-start.70 = (bf16[128,768]{1,0:T(8,128)(2,1)S(1)}, bf16[128,768]{1,0:T(8,128)(2,1)S(1)}, u32[]{:S(2)}, u32[]{:S(2)}) collective-permute-start(bf16[128,768]{1,0:T(8,128)(2,1)S(1)} %grad_add.6.refs_1_), channel_id=1, source_target_pairs={{0,1},{1,0},{2,3},{3,2},{4,5},{5,4},{6,7},{7,6},{8,9},{9,8},{10,11... | collective-permute-start | bytes 589832 | tf_op jit(solution)/shard_map/ppermute | solution.py:666
  442.7 21.5 %collective-permute-start.72 = (bf16[96,768]{1,0:T(8,128)(2,1)S(1)}, bf16[96,768]{1,0:T(8,128)(2,1)S(1)}, u32[]{:S(2)}, u32[]{:S(2)}) collective-permute-start(bf16[96,768]{1,0:T(8,128)(2,1)S(1)} %grad_add.7.refs_1_), channel_id=1, source_target_pairs={{0,2},{1,3},{2,0},{3,1},{4,6},{5,7},{6,4},{7,5},{8,10},{9,11},{10,... | collective-permute-start | bytes 442376 | tf_op jit(solution)/shard_map/ppermute | solution.py:666
  444.7 20.8 %collective-permute-start.71 = (bf16[96,768]{1,0:T(8,128)(2,1)S(1)}, bf16[96,768]{1,0:T(8,128)(2,1)S(1)}, u32[]{:S(2)}, u32[]{:S(2)}) collective-permute-start(bf16[96,768]{1,0:T(8,128)(2,1)S(1)} %grad_add.7.refs_1_), channel_id=1, source_target_pairs={{0,3},{1,2},{2,1},{3,0},{4,7},{5,6},{6,5},{7,4},{8,11},{9,10},{10,... | collective-permute-start | bytes 442376 | tf_op jit(solution)/shard_map/ppermute | solution.py:666
  445.6 31.3 %collective-permute-start.69 = (bf16[128,768]{1,0:T(8,128)(2,1)S(1)}, bf16[128,768]{1,0:T(8,128)(2,1)S(1)}, u32[]{:S(2)}, u32[]{:S(2)}) collective-permute-start(bf16[128,768]{1,0:T(8,128)(2,1)S(1)} %grad_add.6.refs_1_), channel_id=1, source_target_pairs={{0,2},{1,3},{2,0},{3,1},{4,6},{5,7},{6,4},{7,5},{8,10},{9,11},{10,... | collective-permute-start | bytes 589832 | tf_op jit(solution)/shard_map/ppermute | solution.py:666
  446.6 30.3 %collective-permute-start.68 = (bf16[128,768]{1,0:T(8,128)(2,1)S(1)}, bf16[128,768]{1,0:T(8,128)(2,1)S(1)}, u32[]{:S(2)}, u32[]{:S(2)}) collective-permute-start(bf16[128,768]{1,0:T(8,128)(2,1)S(1)} %grad_add.6.refs_1_), channel_id=1, source_target_pairs={{0,3},{1,2},{2,1},{3,0},{4,7},{5,6},{6,5},{7,4},{8,11},{9,10},{10,... | collective-permute-start | bytes 589832 | tf_op jit(solution)/shard_map/ppermute | solution.py:666
  464.2 13.9 %collective-permute-start.56 = (bf16[80,768]{1,0:T(8,128)(2,1)S(1)}, bf16[80,768]{1,0:T(8,128)(2,1)S(1)}, u32[]{:S(2)}, u32[]{:S(2)}) collective-permute-start(bf16[80,768]{1,0:T(8,128)(2,1)S(1)} %get-tuple-element.298), channel_id=1, source_target_pairs={{0,3},{1,2},{2,1},{3,0},{4,7},{5,6},{6,5},{7,4},{8,11},{9,10},{10,... | collective-permute-start | bytes 368648 | tf_op jit(solution)/shard_map/ppermute | solution.py:666
  465.5 19.2 %collective-permute-start.57 = (bf16[80,768]{1,0:T(8,128)(2,1)S(1)}, bf16[80,768]{1,0:T(8,128)(2,1)S(1)}, u32[]{:S(2)}, u32[]{:S(2)}) collective-permute-start(bf16[80,768]{1,0:T(8,128)(2,1)S(1)} %get-tuple-element.299), channel_id=1, source_target_pairs={{0,2},{1,3},{2,0},{3,1},{4,6},{5,7},{6,4},{7,5},{8,10},{9,11},{10,... | collective-permute-start | bytes 368648 | tf_op jit(solution)/shard_map/ppermute | solution.py:666
  469.4 15.3 %collective-permute-start.58 = (bf16[80,768]{1,0:T(8,128)(2,1)S(1)}, bf16[80,768]{1,0:T(8,128)(2,1)S(1)}, u32[]{:S(2)}, u32[]{:S(2)}) collective-permute-start(bf16[80,768]{1,0:T(8,128)(2,1)S(1)} %get-tuple-element.300), channel_id=1, source_target_pairs={{0,1},{1,0},{2,3},{3,2},{4,5},{5,4},{6,7},{7,6},{8,9},{9,8},{10,11... | collective-permute-start | bytes 368648 | tf_op jit(solution)/shard_map/ppermute | solution.py:666
  484.7 10.6 %collective-permute-start.61 = (bf16[80,768]{1,0:T(8,128)(2,1)S(1)}, bf16[80,768]{1,0:T(8,128)(2,1)S(1)}, u32[]{:S(2)}, u32[]{:S(2)}) collective-permute-start(bf16[80,768]{1,0:T(8,128)(2,1)S(1)} %grad_add.5.refs_1_), channel_id=1, source_target_pairs={{0,1},{1,0},{2,3},{3,2},{4,5},{5,4},{6,7},{7,6},{8,9},{9,8},{10,11... | collective-permute-start | bytes 368648 | tf_op jit(solution)/shard_map/ppermute | solution.py:666
  484.8 11.2 %collective-permute-start.60 = (bf16[80,768]{1,0:T(8,128)(2,1)S(1)}, bf16[80,768]{1,0:T(8,128)(2,1)S(1)}, u32[]{:S(2)}, u32[]{:S(2)}) collective-permute-start(bf16[80,768]{1,0:T(8,128)(2,1)S(1)} %grad_add.5.refs_1_), channel_id=1, source_target_pairs={{0,2},{1,3},{2,0},{3,1},{4,6},{5,7},{6,4},{7,5},{8,10},{9,11},{10,... | collective-permute-start | bytes 368648 | tf_op jit(solution)/shard_map/ppermute | solution.py:666
  487.2 8.8 %collective-permute-start.59 = (bf16[80,768]{1,0:T(8,128)(2,1)S(1)}, bf16[80,768]{1,0:T(8,128)(2,1)S(1)}, u32[]{:S(2)}, u32[]{:S(2)}) collective-permute-start(bf16[80,768]{1,0:T(8,128)(2,1)S(1)} %grad_add.5.refs_1_), channel_id=1, source_target_pairs={{0,3},{1,2},{2,1},{3,0},{4,7},{5,6},{6,5},{7,4},{8,11},{9,10},{10,... | collective-permute-start | bytes 368648 | tf_op jit(solution)/shard_map/ppermute | solution.py:666
  (81 other events, 747.6 us)
